TPU v7x, 256 devices: a whole 4x4x8 slice. The times are simulated.
256 devices in a mesh: ka: 16 (over z_lo, x, core), vert: 16 (over y, z_hi).
Axes of the slice: x: 4, y: 4, z: 8 (z_hi: 4, z_lo: 2; z = z_hi * 2 + z_lo), core: 2. Of those that a mesh axis runs over, the one named last changes fastest.
Arguments:
- left_factor: bfloat16 [16, 1, 512, 176, 176], P('ka', None, 'vert'), may hold values from -0.4375 to 0.4375
- right_factor: bfloat16 [16, 1, 512, 176, 176], P('ka', None, 'vert'), may hold values from -0.109375 to 0.109375
- amplitudes: bfloat16 [16, 1, 176, 176], replicated, may hold values from -6 to 6
- kb_table: int32 [16], replicated, may hold values from 0 to 15, as said below
- pair_list: int32 [16, 2], replicated, may hold values from 0 to 31
- occ_energy: float32 [32], replicated, may hold values from -2 to -0.5
- vir_energy: float32 [16, 176], replicated, may hold values from 0.5 to 3
Outputs:
- doubles_update: float32 [16, 176, 16, 176], P('ka', 'vert')
Inputs may be any that keep to these rules, and one draw needn't show every extreme that they name: kb_table[k] = (16 + kij - k) mod 16 for one pair momentum kij, so every sector appears once.
All inputs are finite; a program needn't handle non-finite values.
Results may differ from a plain program's by a relative error of at most 0.0029.
Values may be sent and summed in bfloat16 or wider, within the bound.
A program may use at most 192 MiB of HBM per device.

v0:
```python
import jax
import jax.numpy as jnp
from jax import lax
from jax.sharding import PartitionSpec as P


def on_device(left_factor, right_factor, amplitudes, kb_table, pair_list, occ_energy, vir_energy):
    sector = lax.axis_index("ka")
    sectors = lax.axis_size("ka")
    column = lax.axis_index("vert")
    b_rows = right_factor.shape[3] // lax.axis_size("vert")
    partner = kb_table[sector]
    spread = lax.all_to_all(right_factor, "ka", split_axis=3, concat_axis=0, tiled=True)
    chosen = jnp.take(spread, kb_table, axis=0)
    matched = lax.all_to_all(chosen, "ka", split_axis=0, concat_axis=3, tiled=True)
    half_step = jnp.einsum(
        "slac,pscd->pslad", left_factor[0], amplitudes, preferred_element_type=jnp.float32
    ).astype(jnp.bfloat16)
    partner_rows = matched[0]
    ladder = lax.psum_scatter(
        jnp.einsum("pslad,slbd->bpa", half_step, partner_rows, preferred_element_type=jnp.float32),
        "vert",
        scatter_dimension=0,
        tiled=True,
    )
    occ_ids = jnp.arange(occ_energy.shape[0], dtype=jnp.int32)
    onehot = pair_list[:, :, None] == occ_ids[None, None, :]
    pair_energy = jnp.sum(jnp.where(onehot, occ_energy[None, None, :], 0.0), axis=(1, 2))
    sector_ids = jnp.arange(sectors, dtype=jnp.int32)
    partner_vir = jnp.sum(jnp.where((sector_ids == partner)[:, None], vir_energy, 0.0), axis=0)
    own_vir = jnp.sum(jnp.where((sector_ids == sector)[:, None], vir_energy, 0.0), axis=0)
    b_energy = lax.dynamic_slice_in_dim(partner_vir, column * b_rows, b_rows, 0)
    denominator = pair_energy[None, :, None] - b_energy[:, None, None] - own_vir[None, None, :]
    return (ladder / denominator)[None]


def solution(mesh):
    placed = (
        P("ka", None, "vert", None, None),
        P("ka", None, "vert", None, None),
        P(),
        P(),
        P(),
        P(),
        P(),
    )
    return jax.shard_map(
        on_device,
        mesh=mesh,
        in_specs=placed,
        out_specs=P("ka", "vert", None, None),
        check_vma=False,
    )
```

profile of v0, /device:TPU:6, one launch (start us, length us, event | category | flops | bytes accessed | tf_op | source)
XLA Modules:
  0.0 243.8 jit_solution(2028621400827478143)
XLA Ops:
  6.5 0.0 copy-start
  6.5 4.6 %copy.25 = bf16[1,1,32,176,176]{4,2,1,0,3:T(8,128)(2,1)} copy(bf16[1,1,32,176,176]{4,3,2,1,0:T(8,128)(2,1)} %param.8) | data formatting | bytes 3964928 | tf_op args[1]
  11.1 0.0 copy-start.5
  11.1 6.6 %all-to-all-start = ((bf16[1,1,32,176,176]{4,2,1,0,3:T(8,128)(2,1)}), bf16[1,1,32,176,176]{4,2,1,0,3:T(8,128)(2,1)}, u32[]{:S(2)}, u32[]{:S(2)}) async-start(bf16[1,1,32,176,176]{4,2,1,0,3:T(8,128)(2,1)} %copy.25), calls=%async_computation | async-start | bytes 5767168 | tf_op jit(solution)/shard_map/all_to_all | solution.py:13
  17.7 0.0 copy-done.5
  17.8 41.5 %all-to-all-done = bf16[1,1,32,176,176]{4,2,1,0,3:T(8,128)(2,1)} async-done(((bf16[1,1,32,176,176]{4,2,1,0,3:T(8,128)(2,1)}), bf16[1,1,32,176,176]{4,2,1,0,3:T(8,128)(2,1)}, u32[]{:S(2)}, u32[]{:S(2)}) %all-to-all-start) | async-done | bytes 1982496 | tf_op jit(solution)/shard_map/all_to_all | solution.py:13
  59.2 4.1 %gather_fusion = bf16[16,32,11,176]{3,1,2,0:T(8,128)(2,1)} fusion(bf16[16,32,11,176]{3,1,2,0:T(8,128)(2,1)} %bitcast.2, s32[1024]{0:T(1024)S(1)} %pad_clamp_fusion), kind=kCustom, calls=%fused_computation | custom fusion | bytes 3964992 | tf_op jit(solution)/shard_map/jit(_take)/gather | solution.py:14
  63.3 3.7 %fusion.8 = bf16[16,1,32,11,176]{4,2,3,1,0:T(8,128)(2,1)} fusion(bf16[16,32,11,176]{3,1,2,0:T(8,128)(2,1)} %gather_fusion, pred[16]{0:T(512)(128)(4,1)S(1)} %compare_and_fusion), kind=kLoop, calls=%fused_computation.8 | loop fusion | flops 991232 | bytes 3964944 | tf_op jit(solution)/shard_map/jit(_take)/select_n | solution.py:14
  67.0 4.6 %all-to-all-start.1 = ((bf16[16,1,32,11,176]{4,2,3,1,0:T(8,128)(2,1)}), bf16[16,1,32,11,176]{4,2,3,1,0:T(8,128)(2,1)}, u32[]{:S(2)}, u32[]{:S(2)}) async-start(bf16[16,1,32,11,176]{4,2,3,1,0:T(8,128)(2,1)} %fusion.8), calls=%async_computation.1 | async-start | bytes 5767168 | tf_op jit(solution)/shard_map/all_to_all | solution.py:15
  71.6 0.2 reduce-scatter.2.cloned.1.call-start
  71.8 0.0 copy-done
  71.8 21.6 %fusion.28 = bf16[16,32,176,176]{2,3,1,0:T(8,128)(2,1)} fusion(bf16[1,1,32,176,176]{4,3,2,1,0:T(8,128)(2,1)S(1)} %copy-done, bf16[16,1,176,176]{3,2,1,0:T(8,128)(2,1)} %param.9), kind=kOutput, calls=%fused_computation.2.clone.clone.clone.1 | convolution fusion | flops 5598478336 | bytes 34693120 | tf_op jit(solution)/shard_map/slac,pscd->pslad/dot_general | solution.py:16
  93.4 19.7 %all-to-all-done.1 = bf16[16,1,32,11,176]{4,2,3,1,0:T(8,128)(2,1)} async-done(((bf16[16,1,32,11,176]{4,2,3,1,0:T(8,128)(2,1)}), bf16[16,1,32,11,176]{4,2,3,1,0:T(8,128)(2,1)}, u32[]{:S(2)}, u32[]{:S(2)}) %all-to-all-start.1) | async-done | bytes 1982496 | tf_op jit(solution)/shard_map/all_to_all | solution.py:15
  113.1 24.3 %fusion.10 = f32[176,16,176]{2,0,1:T(8,128)} fusion(bf16[32,176,176]{2,0,1:T(8,128)(2,1)} %bitcast.7, bf16[16,32,176,176]{2,3,1,0:T(8,128)(2,1)} %fusion.28), kind=kOutput, calls=%fused_computation.10 | convolution fusion | flops 5582618624 | bytes 35684352 | tf_op jit(solution)/shard_map/pslad,slbd->bpa/dot_general | solution.py:21
  137.4 0.0 copy-start.1
  137.4 5.2 %copy.30 = f32[176,16,176]{2,1,0:T(8,128)} copy(f32[176,16,176]{2,0,1:T(8,128)} %fusion.10) | data formatting | bytes 3964928 | tf_op jit(solution)/shard_map/pslad,slbd->bpa/dot_general | solution.py:21
  142.6 0.0 copy-start.2
  142.6 0.0 copy-start.3
  142.6 0.0 copy-start.4
  142.6 0.0 reduce-scatter.2.cloned.1.call-update
  142.7 0.6 dynamic_slice.6
  143.3 0.6 iota_compare_fusion.1
  143.9 0.0 copy-done.2
  143.9 0.1 select_reduce_fusion.1
  144.0 0.1 dynamic_slice.7
  144.1 0.0 copy-done.3
  144.1 0.0 copy-done.4
  144.1 0.2 select_reduce_fusion.2
  144.3 0.1 broadcast_subtract_fusion
  144.4 90.9 %reduce-scatter.2.cloned.1.call-done = f32[11,16,176]{2,1,0:T(8,128)} async-done(((f32[176,16,176]{2,1,0:T(8,128)}), f32[11,16,176]{2,1,0:T(8,128)}) %reduce-scatter.2.cloned.1.call-update) | async-done | bytes 123920 | tf_op jit(solution)/shard_map/reduce_scatter | solution.py:20
  235.3 1.7 divide_bitcast_fusion
  237.0 0.0 copy-done.1
  (3 shorter events, 0.0 us)
Async XLA Ops:
  6.5 65.3 %copy-start = (bf16[1,1,32,176,176]{4,3,2,1,0:T(8,128)(2,1)S(1)}, bf16[1,1,32,176,176]{4,3,2,1,0:T(8,128)(2,1)}, u32[]{:S(2)}) copy-start(bf16[1,1,32,176,176]{4,3,2,1,0:T(8,128)(2,1)} %param.7) | copy-start | bytes 5947396
  11.1 6.6 %copy-start.5 = (s32[16]{0:T(128)S(1)}, s32[16]{0:T(128)}, u32[]{:S(2)}) copy-start(s32[16]{0:T(128)} %param.10) | copy-start | bytes 196
  11.1 48.1 %all-to-all-start = ((bf16[1,1,32,176,176]{4,2,1,0,3:T(8,128)(2,1)}), bf16[1,1,32,176,176]{4,2,1,0,3:T(8,128)(2,1)}, u32[]{:S(2)}, u32[]{:S(2)}) async-start(bf16[1,1,32,176,176]{4,2,1,0,3:T(8,128)(2,1)} %copy.25), calls=%async_computation | async-start | bytes 5767168 | tf_op jit(solution)/shard_map/all_to_all | solution.py:13
  67.0 46.1 %all-to-all-start.1 = ((bf16[16,1,32,11,176]{4,2,3,1,0:T(8,128)(2,1)}), bf16[16,1,32,11,176]{4,2,3,1,0:T(8,128)(2,1)}, u32[]{:S(2)}, u32[]{:S(2)}) async-start(bf16[16,1,32,11,176]{4,2,3,1,0:T(8,128)(2,1)} %fusion.8), calls=%async_computation.1 | async-start | bytes 5767168 | tf_op jit(solution)/shard_map/all_to_all | solution.py:15
  71.6 163.7 %reduce-scatter.2.cloned.1.call-start = ((), (), s32[]{:S(2)}) async-start(), calls=%async_computation.3 | async-start | bytes 3063808 | tf_op jit(solution)/shard_map/reduce_scatter | solution.py:20
  137.4 99.6 %copy-start.1 = (bf16[1,1,32,176,176]{4,3,2,1,0:T(8,128)(2,1)S(1)}, bf16[1,1,32,176,176]{4,3,2,1,0:T(8,128)(2,1)}, u32[]{:S(2)}) copy-start(bf16[1,1,32,176,176]{4,3,2,1,0:T(8,128)(2,1)} %param.7) | copy-start | bytes 5947396
  142.6 1.3 copy-start.2
  142.6 1.5 copy-start.3
  142.6 1.5 copy-start.4
Sparse Core Ops, SparseCore 0:
  142.8 92.4 reduce-scatter.1
where the time goes:
time: 244 us
  waiting for transfers between devices  152 us (62%)
  matrix products  45.9 us (19%)
  local copies, waits for them, and re-layouts  14.6 us (6%)
  between operations  13.5 us (6%)
  starting transfers between devices  11.3 us (5%)
  other arithmetic  6.39 us (3%)
    reduce_scatter x1, waiting for transfers between devices, on_device(): lax.psum_scatter(jnp.einsum('pslad,slbd->bpa', half_step, partner_rows, p...  90.9 us
    all_to_all x1, waiting for transfers between devices, on_device(): lax.all_to_all(right_factor, 'ka', split_axis=3, concat_axis=0, tiled=True)  41.5 us
    dot_general x1, matrix products, on_device(): jnp.einsum('pslad,slbd->bpa', half_step, partner_rows, preferred_element_...  24.3 us
    dot_general x1, matrix products, on_device(): jnp.einsum('slac,pscd->pslad', left_factor[0], amplitudes, preferred_elem...  21.6 us
    all_to_all x1, waiting for transfers between devices, on_device(): lax.all_to_all(chosen, 'ka', split_axis=0, concat_axis=3, tiled=True)  19.7 us
    all_to_all x1, starting transfers between devices, on_device(): lax.all_to_all(right_factor, 'ka', split_axis=3, concat_axis=0, tiled=True)  6.58 us
    dot_general x1, local copies, waits for them, and re-layouts, on_device(): jnp.einsum('pslad,slbd->bpa', half_step, partner_rows, preferred_element_...  5.21 us
  transfers between devices with their start and end apart: 3, of which 3 were waited for; matrix products, arithmetic and copies ran while one was open for 10% of the time, Pallas kernels for 0%

commit v1 on v0

v1 whole, which is shorter than its diff:
```python
import jax
import jax.numpy as jnp
from jax import lax
from jax.experimental import pallas as pl
from jax.experimental.pallas import tpu as pltpu
from jax.sharding import PartitionSpec as P

MESH = pl.DeviceIdType.MESH
F32 = jnp.float32
BF16 = jnp.bfloat16

V = 176
AUX = 32
PAIRS = 16
SECTORS = 16
GROUP = 8
GROUPS = AUX // GROUP
GL = GROUP * V
KL = AUX * V
PA = PAIRS * V
HALF = PA // 2
QP = 4
R0, R1 = 8, 3
N0, N1 = 16 * R0, 16 * R1
CHIPS = 8
W1 = 384


def kernel(kb_ref, l_hbm, r_hbm, t_hbm, o_ref,
           l_v, r_v, t_v, t_cat, send0, send1, mid_a, mid_b, mid_c, out0, out1, recv0, recv1, h, acc0, acc1,
           full0, ysend0, yrecv0, sum0, zsend0, zrecv0,
           full1, ysend1, yrecv1, zsend1, zrecv1,
           in_sem, ps_sem, pr_sem, qs_sem, qr_sem, ys_sem, yr_sem, zs_sem, zr_sem):
    me = lax.axis_index("ka")
    vert = lax.axis_index("vert")
    chip, core = me // 2, me % 2
    y, z = vert // 4, vert % 4
    y_peers = [(me, lax.rem(y + s, 4) * 4 + z) for s in (1, 2, 3)]
    z_peers = [(me, y * 4 + lax.rem(z + s, 4)) for s in (1, 2, 3)]

    def r_in(g):
        return pltpu.make_async_copy(r_hbm.at[pl.ds(g * GROUP, GROUP)], r_v.at[pl.ds(g * GROUP, GROUP)], in_sem.at[g])

    def l_in(g):
        rows = pl.ds(pl.multiple_of(g * GL, 16), GL)
        return pltpu.make_async_copy(l_hbm.at[rows], l_v.at[rows], in_sem.at[GROUPS + g])

    t_in = pltpu.make_async_copy(t_hbm, t_v, in_sem.at[2 * GROUPS])
    for g in range(GROUPS):
        r_in(g).start()
    t_in.start()
    for g in range(GROUPS):
        l_in(g).start()

    barrier = pltpu.get_barrier_semaphore()
    for peer in y_peers + z_peers:
        pl.semaphore_signal(barrier, inc=1, device_id=peer, device_id_type=MESH)

    @pl.loop(1, SECTORS)
    def _(s):
        pl.semaphore_signal(barrier, inc=1, device_id=(lax.rem(me + s, SECTORS), vert), device_id_type=MESH)

    mids = (mid_a, mid_b, mid_c)

    row = lax.broadcasted_iota(jnp.int32, (V, V), 0)
    col = lax.broadcasted_iota(jnp.int32, (V, V), 1)
    late = row - N0
    third = lax.shift_right_logical(late * 21846, 16)
    source = jnp.where(row < N0, 11 * lax.shift_right_logical(row, 3) + (row & 7), 11 * third + R0 + (late - 3 * third))
    order = (col == source).astype(F32).astype(BF16)

    for half in range(2):
        send1[half, :, 2 * GL:] = jnp.zeros((N1, W1 * CHIPS - 2 * GL), BF16)
    pl.semaphore_wait(barrier, SECTORS - 1 + 6)

    def hop(src, dst, send_sem, recv_sem, target, far):
        if far:
            return pltpu.make_async_remote_copy(
                src_ref=src, dst_ref=dst, send_sem=send_sem, recv_sem=recv_sem,
                device_id=(target, vert), device_id_type=MESH,
            )
        return pltpu.make_async_copy(src, dst, recv_sem)

    def first(unit, s, far):
        j = lax.rem(chip + s, CHIPS)
        if unit < GROUPS:
            src = send0.at[pl.ds(pl.multiple_of(16 * j, 16), 16), pl.ds(unit * GL, GL)]
            dst = mids[unit // 2].at[me]
            which = unit // 2
        else:
            src = send1.at[unit - GROUPS, :, pl.ds(pl.multiple_of(W1 * j, 128), W1)]
            dst = mids[2].at[me]
            which = 2
        return hop(src, dst, ps_sem.at[unit, s], pr_sem.at[which], 2 * j + unit % 2, far)

    def second(which, s, t, far):
        j = lax.rem(chip + s, CHIPS)
        k = 2 * j + t
        if which < 2:
            src = out0.at[which, k]
            g = 2 * which + core
            dst = recv0.at[pl.ds(pl.multiple_of(16 * chip, 16), 16), pl.ds(pl.multiple_of(g * GL, 128), GL)]
        else:
            src = out1.at[k]
            g = GROUPS + core
            dst = recv1.at[core, :, pl.ds(pl.multiple_of(W1 * chip, 128), W1)]
        return hop(src, dst, qs_sem.at[which, 2 * s + t], qr_sem.at[g], k, far)

    def start_first(unit):
        @pl.when(core == unit % 2)
        def _():
            first(unit, 0, False).start()

        @pl.when(core != unit % 2)
        def _():
            first(unit, 0, True).start()

        for s in range(1, CHIPS):
            first(unit, s, True).start()

    def start_second(which):
        mid, out = mids[which], out0.at[which] if which < 2 else out1
        pltpu.make_async_copy(mid, mid, pr_sem.at[which]).wait()

        @pl.loop(0, SECTORS)
        def _(k):
            out[k] = mid[kb_ref[k]]

        for s in range(1, CHIPS):
            for t in range(2):
                second(which, s, t, True).start()
        for t in range(2):
            @pl.when(core == t)
            def _():
                second(which, 0, t, False).start()

            @pl.when(core != t)
            def _():
                second(which, 0, t, True).start()

    for g in range(GROUPS):
        r_in(g).wait()
        parts = [jnp.dot(order, r_v[g * GROUP + i], preferred_element_type=F32).astype(BF16) for i in range(GROUP)]
        packed = jnp.concatenate(parts, axis=1)
        send0[:, g * GL:(g + 1) * GL] = packed[:N0]
        send1[g // 2, :, (g % 2) * GL:(g % 2 + 1) * GL] = packed[N0:]
        start_first(g)
    for half in range(2):
        start_first(GROUPS + half)

    t_in.wait()
    for q in range(PAIRS // QP):
        t_cat[q] = jnp.concatenate([t_v[q * QP + i] for i in range(QP)], axis=1)

    @pl.loop(0, GROUPS)
    def _(g):
        l_in(g).wait()

        @pl.loop(0, PAIRS // QP)
        def _(q):
            amps = t_cat[q]
            outs = []
            for i in range(GROUP):
                rows = pl.ds(pl.multiple_of(g * GL + i * V, 16), V)
                outs.append(jnp.dot(l_v[rows, :], amps, preferred_element_type=F32).astype(BF16))
            for i in range(QP):
                rows = pl.ds(pl.multiple_of(q * QP * V + i * V, 16), V)
                h[rows, pl.ds(pl.multiple_of(g * GL, 128), GL)] = jnp.concatenate(
                    [o[:, i * V:(i + 1) * V] for o in outs], axis=1
                )

        @pl.when(g == GROUPS - 2)
        def _():
            start_second(0)

    start_second(1)
    start_second(2)

    def add(acc, right, g):
        lanes = pl.ds(pl.multiple_of(g * GL, 128), GL)

        @pl.loop(0, 4)
        def _(m):
            rows = pl.ds(pl.multiple_of(m * (PA // 4), 16), PA // 4)
            acc[rows, :] += lax.dot_general(
                h[rows, lanes], right[...], (((1,), (1,)), ((), ())), preferred_element_type=F32
            )

    def add0(g):
        part = recv0.at[:, pl.ds(pl.multiple_of(g * GL, 128), GL)]
        pltpu.make_async_copy(part, part, qr_sem.at[g]).wait()
        add(acc0, part, g)

    def add1(g):
        half = g // 2

        @pl.when(lax.rem(g, 2) == 0)
        def _():
            pltpu.make_async_copy(recv1.at[half], recv1.at[half], qr_sem.at[GROUPS + half]).wait()

        add(acc1, recv1.at[half, :, pl.ds(pl.multiple_of(lax.rem(g, 2) * GL, 128), GL)], g)

    acc0[...] = jnp.zeros_like(acc0)
    acc1[...] = jnp.zeros_like(acc1)
    full1[...] = jnp.zeros_like(full1)
    zsend1[...] = jnp.zeros_like(zsend1)

    @pl.loop(0, GROUPS)
    def _(g):
        add0(g)

    def y_copy(chunk, s):
        src, dst = (ysend0, yrecv0) if chunk == 0 else (ysend1, yrecv1)
        return pltpu.make_async_remote_copy(
            src_ref=src.at[lax.rem(y + s, 4)], dst_ref=dst.at[s - 1],
            send_sem=ys_sem.at[chunk, s - 1], recv_sem=yr_sem.at[chunk, s - 1],
            device_id=y_peers[s - 1], device_id_type=MESH,
        )

    def z_copy(chunk, s):
        src, dst = (zsend0, zrecv0) if chunk == 0 else (zsend1, zrecv1)
        return pltpu.make_async_remote_copy(
            src_ref=src.at[lax.rem(z + s, 4)], dst_ref=dst.at[s - 1],
            send_sem=zs_sem.at[chunk, s - 1], recv_sem=zr_sem.at[chunk, s - 1],
            device_id=z_peers[s - 1], device_id_type=MESH,
        )

    @pl.loop(0, PA // 128)
    def _(m):
        at = pl.ds(pl.multiple_of(m * 128, 128), 128)
        turned = acc0[at, :].T
        full0[:, at] = turned
        for j in range(4):
            ysend0[j, :, at] = turned[32 * j:32 * (j + 1)].astype(BF16)

    for s in (1, 2, 3):
        y_copy(0, s).start()

    @pl.loop(0, GROUPS - 1)
    def _(g):
        add1(g)

    for s in (1, 2, 3):
        y_copy(0, s).wait()
    total = full0[pl.ds(pl.multiple_of(32 * y, 8), 32), :]
    for s in range(3):
        total = total + yrecv0[s].astype(F32)
    sum0[...] = total
    for j in range(4):
        part = sum0[8 * j:8 * (j + 1), :]
        zsend0[j] = jnp.concatenate([part[:, :HALF], part[:, HALF:]], axis=0).astype(BF16)
    for s in (1, 2, 3):
        z_copy(0, s).start()

    add1(jnp.int32(GROUPS - 1))

    @pl.loop(0, PA // 128)
    def _(m):
        at = pl.ds(pl.multiple_of(m * 128, 128), 128)
        turned = acc1[at, :].T
        for j in range(4):
            full1[j, 0:12, at] = turned[12 * j:12 * (j + 1)]
    for j in range(4):
        ysend1[j] = full1[j].astype(BF16)
    for s in (1, 2, 3):
        y_copy(1, s).start()

    for s in (1, 2, 3):
        z_copy(0, s).wait()
    own = sum0[pl.ds(pl.multiple_of(8 * z, 8), 8), :]
    low, high = own[:, :HALF], own[:, HALF:]
    for s in range(3):
        got = zrecv0[s].astype(F32)
        low, high = low + got[0:8], high + got[8:16]
    o_ref[0:8, :HALF] = low
    o_ref[0:8, HALF:] = high

    for s in (1, 2, 3):
        y_copy(1, s).wait()
    rest = full1[y]
    for s in range(3):
        rest = rest + yrecv1[s].astype(F32)
    for j in range(4):
        zsend1[j, 0:3, :] = rest[3 * j:3 * j + 3, :HALF]
        zsend1[j, 4:7, :] = rest[3 * j:3 * j + 3, HALF:]
    for s in (1, 2, 3):
        z_copy(1, s).start()
    for s in (1, 2, 3):
        z_copy(1, s).wait()
    last = zsend1[z]
    for s in range(3):
        last = last + zrecv1[s]
    o_ref[8:16, :HALF] = last
    o_ref[8:12, HALF:] = last[4:8]
    o_ref[12:16, HALF:] = last[4:8]

    for unit in range(GROUPS + 2):
        @pl.when(core != unit % 2)
        def _():
            first(unit, 0, True).wait_send()

        for s in range(1, CHIPS):
            first(unit, s, True).wait_send()
    for which in range(3):
        for t in range(2):
            @pl.when(core != t)
            def _():
                second(which, 0, t, True).wait_send()

            for s in range(1, CHIPS):
                second(which, s, t, True).wait_send()


def ladder_of(kb_table, left, right, amps):
    any_space = pl.BlockSpec(memory_space=pl.ANY)
    vmem = pltpu.VMEM
    return pl.pallas_call(
        kernel,
        out_shape=jax.ShapeDtypeStruct((16, PA), F32),
        in_specs=[pl.BlockSpec(memory_space=pltpu.SMEM)] + [any_space] * 3,
        out_specs=pl.BlockSpec(memory_space=pltpu.VMEM),
        scratch_shapes=[
            vmem((KL, V), BF16), vmem((AUX, V, V), BF16), vmem((PAIRS, V, V), BF16),
            vmem((PAIRS // QP, V, QP * V), BF16),
            vmem((N0, KL), BF16), vmem((2, N1, W1 * CHIPS), BF16),
            vmem((SECTORS, 16, GL), BF16), vmem((SECTORS, 16, GL), BF16), vmem((SECTORS, N1, W1), BF16),
            vmem((2, SECTORS, 16, GL), BF16), vmem((SECTORS, N1, W1), BF16),
            vmem((N0, KL), BF16), vmem((2, N1, W1 * CHIPS), BF16), vmem((PA, KL), BF16),
            vmem((PA, N0), F32), vmem((PA, N1), F32),
            vmem((N0, PA), F32), vmem((4, 32, PA), BF16), vmem((3, 32, PA), BF16),
            vmem((32, PA), F32), vmem((4, 16, HALF), BF16), vmem((3, 16, HALF), BF16),
            vmem((4, 16, PA), F32), vmem((4, 16, PA), BF16), vmem((3, 16, PA), BF16),
            vmem((4, 8, HALF), F32), vmem((3, 8, HALF), F32),
            pltpu.SemaphoreType.DMA((2 * GROUPS + 1,)),
            pltpu.SemaphoreType.DMA((GROUPS + 2, CHIPS)), pltpu.SemaphoreType.DMA((3,)),
            pltpu.SemaphoreType.DMA((3, SECTORS)), pltpu.SemaphoreType.DMA((GROUPS + 2,)),
            pltpu.SemaphoreType.DMA((2, 3)), pltpu.SemaphoreType.DMA((2, 3)),
            pltpu.SemaphoreType.DMA((2, 3)), pltpu.SemaphoreType.DMA((2, 3)),
        ],
        compiler_params=pltpu.CompilerParams(
            collective_id=0, has_side_effects=True, vmem_limit_bytes=60 * 2**20
        ),
    )(kb_table, left, right, amps)


def on_device(left_factor, right_factor, amplitudes, kb_table, pair_list, occ_energy, vir_energy):
    sector = lax.axis_index("ka")
    sectors = lax.axis_size("ka")
    column = lax.axis_index("vert")
    b_rows = V // lax.axis_size("vert")
    partner = kb_table[sector]
    left = left_factor.reshape(KL, V)
    right = right_factor.reshape(AUX, V, V)
    amps = amplitudes.reshape(PAIRS, V, V)
    ladder = ladder_of(kb_table, left, right, amps)[:b_rows].reshape(b_rows, PAIRS, V)
    occ_ids = jnp.arange(occ_energy.shape[0], dtype=jnp.int32)
    onehot = pair_list[:, :, None] == occ_ids[None, None, :]
    pair_energy = jnp.sum(jnp.where(onehot, occ_energy[None, None, :], 0.0), axis=(1, 2))
    sector_ids = jnp.arange(sectors, dtype=jnp.int32)
    partner_vir = jnp.sum(jnp.where((sector_ids == partner)[:, None], vir_energy, 0.0), axis=0)
    own_vir = jnp.sum(jnp.where((sector_ids == sector)[:, None], vir_energy, 0.0), axis=0)
    b_energy = lax.dynamic_slice_in_dim(partner_vir, column * b_rows, b_rows, 0)
    denominator = pair_energy[None, :, None] - b_energy[:, None, None] - own_vir[None, None, :]
    return (ladder / denominator)[None]


def solution(mesh):
    placed = (
        P("ka", None, "vert", None, None),
        P("ka", None, "vert", None, None),
        P(),
        P(),
        P(),
        P(),
        P(),
    )
    return jax.shard_map(
        on_device,
        mesh=mesh,
        in_specs=placed,
        out_specs=P("ka", "vert", None, None),
        check_vma=False,
    )
```

time: 244 us -> 92.8 us (0.38)
  waiting for transfers between devices: 152 us -> 0 us
  Pallas kernels: 0 us -> 89 us
  matrix products: 45.9 us -> 0 us
  between operations: 13.5 us -> 0.06 us
  local copies, waits for them, and re-layouts: 14.6 us -> 1.75 us
  starting transfers between devices: 11.3 us -> 0 us
  other arithmetic: 6.39 us -> 1.78 us
    reduce_scatter x1 -> x0, waiting for transfers between devices: 90.9 us -> none  [on_device(): lax.psum_scatter(jnp.einsum('pslad,slbd->bpa', half_step, partner_rows, p...]
    pallas_call x0 -> x1, Pallas kernels: none -> 89 us  [ladder_of(): pl.pallas_call(kernel, out_shape=jax.ShapeDtypeStruct((16, PA), F32), in_...]
    all_to_all x2 -> x0, waiting for transfers between devices: 61.2 us -> none  [the longest x1 41.5 us: on_device(): lax.all_to_all(right_factor, 'ka', split_axis=3, concat_axis=0, tiled=True)]
    dot_general x2 -> x0, matrix products: 45.9 us -> none  [the longest x1 24.3 us: on_device(): jnp.einsum('pslad,slbd->bpa', half_step, partner_rows, preferred_element_...]
    all_to_all x2 -> x0, starting transfers between devices: 11.1 us -> none  [the longest x1 6.58 us: on_device(): lax.all_to_all(right_factor, 'ka', split_axis=3, concat_axis=0, tiled=True)]
    dot_general x1 -> x0, local copies, waits for them, and re-layouts: 5.21 us -> none  [on_device(): jnp.einsum('pslad,slbd->bpa', half_step, partner_rows, preferred_element_...]
    unnamed x13 -> x8, local copies, waits for them, and re-layouts: 4.61 us -> 0.02 us
    gather x1 -> x0, local copies, waits for them, and re-layouts: 4.07 us -> none  [on_device(): chosen = jnp.take(spread, kb_table, axis=0)]
  transfers between devices with their start and end apart: 3 -> 0, of which waited for: 3 -> 0; matrix products, arithmetic and copies ran while one was open for 10% -> 0% of each run, Pallas kernels for 0% -> 0%
where the time goes in v1:
time: 92.8 us; the launch traced here: 92.6 us
  Pallas kernels  89 us (96%)
  other arithmetic  1.78 us (2%)
  local copies, waits for them, and re-layouts  1.75 us (2%)
    pallas_call x1, Pallas kernels, ladder_of(): pl.pallas_call(kernel, out_shape=jax.ShapeDtypeStruct((16, PA), F32), in_...  89 us

profile of v1, /device:TPU:6, one launch (start us, length us, event | category | flops | bytes accessed | tf_op | source)
XLA Modules:
  0.0 92.6 jit_solution(12896908920838620344)
XLA Ops:
  0.0 0.0 copy-start.3
  0.0 0.0 copy-start
  0.0 0.0 copy-start.1
  0.0 0.0 copy-start.2
  0.0 89.0 %shard_map.73 = f32[16,2816]{1,0:T(8,128)} custom-call(s32[16]{0:T(128)} %kb_ref.1, bf16[5632,176]{1,0:T(8,128)(2,1)} %bitcast.5, bf16[32,176,176]{2,1,0:T(8,128)(2,1)} %bitcast.6, bf16[16,176,176]{2,1,0:T(8,128)(2,1)} %bitcast.7), custom_call_target="tpu_custom_call" | custom-call | tf_op jit(solution)/shard_map/pallas_call | solution.py:317
  89.1 1.1 %reshape.71 = f32[1,11,16,176]{3,2,1,0:T(8,128)S(1)} reshape(f32[11,2816]{1,0:T(8,128)} %bitcast.8) | data formatting | bytes 247808 | tf_op jit(solution)/shard_map/reshape | solution.py:355
  90.1 0.0 copy-done.3
  90.1 0.6 dynamic_slice.6
  90.7 0.6 iota_compare_fusion.1
  91.4 0.0 copy-done
  91.4 0.1 select_reduce_fusion.1
  91.5 0.1 dynamic_slice.7
  91.6 0.0 copy-done.1
  91.6 0.0 copy-done.2
  91.6 0.2 select_reduce_fusion.2
  91.8 0.1 broadcast_subtract_fusion
  91.8 0.8 subtract_divide_fusion
Async XLA Ops:
  0.0 90.1 %copy-start.3 = (s32[16]{0:T(128)S(1)}, s32[16]{0:T(128)}, u32[]{:S(2)}) copy-start(s32[16]{0:T(128)} %kb_ref.1) | copy-start | bytes 196
  0.0 91.4 %copy-start = (f32[16,176]{1,0:T(8,128)S(1)}, f32[16,176]{1,0:T(8,128)}, u32[]{:S(2)}) copy-start(f32[16,176]{1,0:T(8,128)} %param.13) | copy-start | bytes 33796
  0.0 91.6 %copy-start.1 = (s32[16,2]{0,1:T(2,128)S(1)}, s32[16,2]{0,1:T(2,128)}, u32[]{:S(2)}) copy-start(s32[16,2]{0,1:T(2,128)} %param.11) | copy-start | bytes 388
  0.0 91.6 %copy-start.2 = (f32[32]{0:T(128)S(1)}, f32[32]{0:T(128)}, u32[]{:S(2)}) copy-start(f32[32]{0:T(128)} %param.12) | copy-start | bytes 388

commit v2 on v1

--- a/solution.py
+++ b/solution.py
@@ -23,11 +23,12 @@
 R0, R1 = 8, 3
 N0, N1 = 16 * R0, 16 * R1
 CHIPS = 8
+W2 = 768
 W1 = 384
 
 
-def kernel(kb_ref, l_hbm, r_hbm, t_hbm, o_ref,
-           l_v, r_v, t_v, t_cat, send0, send1, mid_a, mid_b, mid_c, out0, out1, recv0, recv1, h, acc0, acc1,
+def kernel(kb_ref, pair_ref, occ_ref, vir_ref, own_vir_ref, l_hbm, r_hbm, t_hbm, o_ref,
+           l_v, r_v, t_v, t_cat, send0, send1, mid_a, mid_b, mid_c, out0, out1, recv0, recv1, h, acc0, acc1, den,
            full0, ysend0, yrecv0, sum0, zsend0, zrecv0,
            full1, ysend1, yrecv1, zsend1, zrecv1,
            in_sem, ps_sem, pr_sem, qs_sem, qr_sem, ys_sem, yr_sem, zs_sem, zr_sem):
@@ -71,7 +72,6 @@
 
     for half in range(2):
         send1[half, :, 2 * GL:] = jnp.zeros((N1, W1 * CHIPS - 2 * GL), BF16)
-    pl.semaphore_wait(barrier, SECTORS - 1 + 6)
 
     def hop(src, dst, send_sem, recv_sem, target, far):
         if far:
@@ -144,9 +144,19 @@
         packed = jnp.concatenate(parts, axis=1)
         send0[:, g * GL:(g + 1) * GL] = packed[:N0]
         send1[g // 2, :, (g % 2) * GL:(g % 2 + 1) * GL] = packed[N0:]
+        if g == 0:
+            pl.semaphore_wait(barrier, SECTORS - 1 + 6)
         start_first(g)
     for half in range(2):
         start_first(GROUPS + half)
+
+    pair_row = jnp.concatenate(
+        [jnp.full((1, V), occ_ref[pair_ref[p, 0]] + occ_ref[pair_ref[p, 1]], F32) for p in range(PAIRS)], axis=1
+    )
+    own_vir = own_vir_ref[pl.ds(me, 1), :]
+    own_row = jnp.concatenate([own_vir] * PAIRS, axis=1)
+    for r in range(R0 + R1):
+        den[r:r + 1, :] = (pair_row - vir_ref[kb_ref[me], (R0 + R1) * vert + r]) - own_row
 
     t_in.wait()
     for q in range(PAIRS // QP):
@@ -169,59 +179,52 @@
                     [o[:, i * V:(i + 1) * V] for o in outs], axis=1
                 )
 
-        @pl.when(g == GROUPS - 2)
+        @pl.when(g == GROUPS // 2 - 1)
         def _():
             start_second(0)
 
     start_second(1)
-    start_second(2)
-
-    def add(acc, right, g):
-        lanes = pl.ds(pl.multiple_of(g * GL, 128), GL)
+
+    def add(acc, right, half):
+        lanes = pl.ds(half * 2 * GL, 2 * GL)
 
         @pl.loop(0, 4)
         def _(m):
             rows = pl.ds(pl.multiple_of(m * (PA // 4), 16), PA // 4)
-            acc[rows, :] += lax.dot_general(
+            term = lax.dot_general(
                 h[rows, lanes], right[...], (((1,), (1,)), ((), ())), preferred_element_type=F32
             )
-
-    def add0(g):
-        part = recv0.at[:, pl.ds(pl.multiple_of(g * GL, 128), GL)]
-        pltpu.make_async_copy(part, part, qr_sem.at[g]).wait()
-        add(acc0, part, g)
-
-    def add1(g):
-        half = g // 2
-
-        @pl.when(lax.rem(g, 2) == 0)
-        def _():
-            pltpu.make_async_copy(recv1.at[half], recv1.at[half], qr_sem.at[GROUPS + half]).wait()
-
-        add(acc1, recv1.at[half, :, pl.ds(pl.multiple_of(lax.rem(g, 2) * GL, 128), GL)], g)
-
-    acc0[...] = jnp.zeros_like(acc0)
-    acc1[...] = jnp.zeros_like(acc1)
+            acc[rows, :] = term if half == 0 else acc[rows, :] + term
+
+    def add0(half):
+        for g in (2 * half, 2 * half + 1):
+            part = recv0.at[:, pl.ds(g * GL, GL)]
+            pltpu.make_async_copy(part, part, qr_sem.at[g]).wait()
+        add(acc0, recv0.at[:, pl.ds(half * 2 * GL, 2 * GL)], half)
+
+    def add1(half):
+        pltpu.make_async_copy(recv1.at[half], recv1.at[half], qr_sem.at[GROUPS + half]).wait()
+        add(acc1, recv1.at[half, :, pl.ds(0, 2 * GL)], half)
+
     full1[...] = jnp.zeros_like(full1)
     zsend1[...] = jnp.zeros_like(zsend1)
-
-    @pl.loop(0, GROUPS)
-    def _(g):
-        add0(g)
-
-    def y_copy(chunk, s):
-        src, dst = (ysend0, yrecv0) if chunk == 0 else (ysend1, yrecv1)
+    add0(0)
+    start_second(2)
+    add0(1)
+
+    def y_copy(part, s):
+        src, dst = (ysend0, yrecv0) if part == 0 else (ysend1.at[part - 1], yrecv1.at[part - 1])
         return pltpu.make_async_remote_copy(
             src_ref=src.at[lax.rem(y + s, 4)], dst_ref=dst.at[s - 1],
-            send_sem=ys_sem.at[chunk, s - 1], recv_sem=yr_sem.at[chunk, s - 1],
+            send_sem=ys_sem.at[part, s - 1], recv_sem=yr_sem.at[part, s - 1],
             device_id=y_peers[s - 1], device_id_type=MESH,
         )
 
-    def z_copy(chunk, s):
-        src, dst = (zsend0, zrecv0) if chunk == 0 else (zsend1, zrecv1)
+    def z_copy(part, s):
+        src, dst = (zsend0, zrecv0) if part == 0 else (zsend1.at[part - 1], zrecv1.at[part - 1])
         return pltpu.make_async_remote_copy(
             src_ref=src.at[lax.rem(z + s, 4)], dst_ref=dst.at[s - 1],
-            send_sem=zs_sem.at[chunk, s - 1], recv_sem=zr_sem.at[chunk, s - 1],
+            send_sem=zs_sem.at[part, s - 1], recv_sem=zr_sem.at[part, s - 1],
             device_id=z_peers[s - 1], device_id_type=MESH,
         )
 
@@ -236,9 +239,7 @@
     for s in (1, 2, 3):
         y_copy(0, s).start()
 
-    @pl.loop(0, GROUPS - 1)
-    def _(g):
-        add1(g)
+    add1(0)
 
     for s in (1, 2, 3):
         y_copy(0, s).wait()
@@ -252,18 +253,19 @@
     for s in (1, 2, 3):
         z_copy(0, s).start()
 
-    add1(jnp.int32(GROUPS - 1))
-
-    @pl.loop(0, PA // 128)
-    def _(m):
-        at = pl.ds(pl.multiple_of(m * 128, 128), 128)
-        turned = acc1[at, :].T
-        for j in range(4):
-            full1[j, 0:12, at] = turned[12 * j:12 * (j + 1)]
-    for j in range(4):
-        ysend1[j] = full1[j].astype(BF16)
-    for s in (1, 2, 3):
-        y_copy(1, s).start()
+    add1(1)
+
+    for part in (1, 2):
+        @pl.loop(0, HALF // 128)
+        def _(m):
+            at = pl.ds(pl.multiple_of(m * 128, 128), 128)
+            turned = acc1[pl.ds(pl.multiple_of((part - 1) * HALF + m * 128, 128), 128), :].T
+            for j in range(4):
+                full1[part - 1, j, 0:12, at] = turned[12 * j:12 * (j + 1)]
+
+        ysend1[part - 1] = full1[part - 1].astype(BF16)
+        for s in (1, 2, 3):
+            y_copy(part, s).start()
 
     for s in (1, 2, 3):
         z_copy(0, s).wait()
@@ -272,27 +274,29 @@
     for s in range(3):
         got = zrecv0[s].astype(F32)
         low, high = low + got[0:8], high + got[8:16]
-    o_ref[0:8, :HALF] = low
-    o_ref[0:8, HALF:] = high
-
-    for s in (1, 2, 3):
-        y_copy(1, s).wait()
-    rest = full1[y]
-    for s in range(3):
-        rest = rest + yrecv1[s].astype(F32)
-    for j in range(4):
-        zsend1[j, 0:3, :] = rest[3 * j:3 * j + 3, :HALF]
-        zsend1[j, 4:7, :] = rest[3 * j:3 * j + 3, HALF:]
-    for s in (1, 2, 3):
-        z_copy(1, s).start()
-    for s in (1, 2, 3):
-        z_copy(1, s).wait()
-    last = zsend1[z]
-    for s in range(3):
-        last = last + zrecv1[s]
-    o_ref[8:16, :HALF] = last
-    o_ref[8:12, HALF:] = last[4:8]
-    o_ref[12:16, HALF:] = last[4:8]
+    o_ref[0:8, :HALF] = low / den[0:8, :HALF]
+    o_ref[0:8, HALF:] = high / den[0:8, HALF:]
+
+    for part in (1, 2):
+        for s in (1, 2, 3):
+            y_copy(part, s).wait()
+        rest = full1[part - 1, y]
+        for s in range(3):
+            rest = rest + yrecv1[part - 1, s].astype(F32)
+        for j in range(4):
+            zsend1[part - 1, j, 0:3, :] = rest[3 * j:3 * j + 3, :W2]
+            zsend1[part - 1, j, 4:7, :HALF - W2] = rest[3 * j:3 * j + 3, W2:]
+        for s in (1, 2, 3):
+            z_copy(part, s).start()
+    for part in (1, 2):
+        for s in (1, 2, 3):
+            z_copy(part, s).wait()
+        last = zsend1[part - 1, z]
+        for s in range(3):
+            last = last + zrecv1[part - 1, s]
+        at = (part - 1) * HALF
+        o_ref[8:11, at:at + W2] = last[0:3] / den[8:11, at:at + W2]
+        o_ref[8:11, at + W2:at + HALF] = last[4:7, :HALF - W2] / den[8:11, at + W2:at + HALF]
 
     for unit in range(GROUPS + 2):
         @pl.when(core != unit % 2)
@@ -311,13 +315,14 @@
                 second(which, s, t, True).wait_send()
 
 
-def ladder_of(kb_table, left, right, amps):
+def update_of(kb_table, pair_list, occ_energy, vir_energy, left, right, amps):
     any_space = pl.BlockSpec(memory_space=pl.ANY)
+    smem = pl.BlockSpec(memory_space=pltpu.SMEM)
     vmem = pltpu.VMEM
     return pl.pallas_call(
         kernel,
-        out_shape=jax.ShapeDtypeStruct((16, PA), F32),
-        in_specs=[pl.BlockSpec(memory_space=pltpu.SMEM)] + [any_space] * 3,
+        out_shape=jax.ShapeDtypeStruct((R0 + R1, PA), F32),
+        in_specs=[smem] * 4 + [pl.BlockSpec(memory_space=pltpu.VMEM)] + [any_space] * 3,
         out_specs=pl.BlockSpec(memory_space=pltpu.VMEM),
         scratch_shapes=[
             vmem((KL, V), BF16), vmem((AUX, V, V), BF16), vmem((PAIRS, V, V), BF16),
@@ -326,42 +331,29 @@
             vmem((SECTORS, 16, GL), BF16), vmem((SECTORS, 16, GL), BF16), vmem((SECTORS, N1, W1), BF16),
             vmem((2, SECTORS, 16, GL), BF16), vmem((SECTORS, N1, W1), BF16),
             vmem((N0, KL), BF16), vmem((2, N1, W1 * CHIPS), BF16), vmem((PA, KL), BF16),
-            vmem((PA, N0), F32), vmem((PA, N1), F32),
+            vmem((PA, N0), F32), vmem((PA, N1), F32), vmem((16, PA), F32),
             vmem((N0, PA), F32), vmem((4, 32, PA), BF16), vmem((3, 32, PA), BF16),
             vmem((32, PA), F32), vmem((4, 16, HALF), BF16), vmem((3, 16, HALF), BF16),
-            vmem((4, 16, PA), F32), vmem((4, 16, PA), BF16), vmem((3, 16, PA), BF16),
-            vmem((4, 8, HALF), F32), vmem((3, 8, HALF), F32),
+            vmem((2, 4, 16, HALF), F32), vmem((2, 4, 16, HALF), BF16), vmem((2, 3, 16, HALF), BF16),
+            vmem((2, 4, 8, W2), F32), vmem((2, 3, 8, W2), F32),
             pltpu.SemaphoreType.DMA((2 * GROUPS + 1,)),
             pltpu.SemaphoreType.DMA((GROUPS + 2, CHIPS)), pltpu.SemaphoreType.DMA((3,)),
             pltpu.SemaphoreType.DMA((3, SECTORS)), pltpu.SemaphoreType.DMA((GROUPS + 2,)),
-            pltpu.SemaphoreType.DMA((2, 3)), pltpu.SemaphoreType.DMA((2, 3)),
-            pltpu.SemaphoreType.DMA((2, 3)), pltpu.SemaphoreType.DMA((2, 3)),
+            pltpu.SemaphoreType.DMA((3, 3)), pltpu.SemaphoreType.DMA((3, 3)),
+            pltpu.SemaphoreType.DMA((3, 3)), pltpu.SemaphoreType.DMA((3, 3)),
         ],
         compiler_params=pltpu.CompilerParams(
             collective_id=0, has_side_effects=True, vmem_limit_bytes=60 * 2**20
         ),
-    )(kb_table, left, right, amps)
+    )(kb_table, pair_list, occ_energy, vir_energy, vir_energy, left, right, amps)
 
 
 def on_device(left_factor, right_factor, amplitudes, kb_table, pair_list, occ_energy, vir_energy):
-    sector = lax.axis_index("ka")
-    sectors = lax.axis_size("ka")
-    column = lax.axis_index("vert")
-    b_rows = V // lax.axis_size("vert")
-    partner = kb_table[sector]
     left = left_factor.reshape(KL, V)
     right = right_factor.reshape(AUX, V, V)
     amps = amplitudes.reshape(PAIRS, V, V)
-    ladder = ladder_of(kb_table, left, right, amps)[:b_rows].reshape(b_rows, PAIRS, V)
-    occ_ids = jnp.arange(occ_energy.shape[0], dtype=jnp.int32)
-    onehot = pair_list[:, :, None] == occ_ids[None, None, :]
-    pair_energy = jnp.sum(jnp.where(onehot, occ_energy[None, None, :], 0.0), axis=(1, 2))
-    sector_ids = jnp.arange(sectors, dtype=jnp.int32)
-    partner_vir = jnp.sum(jnp.where((sector_ids == partner)[:, None], vir_energy, 0.0), axis=0)
-    own_vir = jnp.sum(jnp.where((sector_ids == sector)[:, None], vir_energy, 0.0), axis=0)
-    b_energy = lax.dynamic_slice_in_dim(partner_vir, column * b_rows, b_rows, 0)
-    denominator = pair_energy[None, :, None] - b_energy[:, None, None] - own_vir[None, None, :]
-    return (ladder / denominator)[None]
+    update = update_of(kb_table, pair_list, occ_energy, vir_energy, left, right, amps)
+    return update.reshape(1, R0 + R1, PAIRS, V)
 
 
 def solution(mesh):

time: 92.8 us -> 91.9 us (level)
  other arithmetic: 1.78 us -> 0 us
  local copies, waits for them, and re-layouts: 1.75 us -> 3.1 us
    unnamed x8 -> x1, local copies, waits for them, and re-layouts: 0.02 us -> 1.35 us
where the time goes in v2:
time: 91.9 us; the launch traced here: 91.7 us
  Pallas kernels  88.6 us (96%)
  local copies, waits for them, and re-layouts  3.1 us (3%)
    pallas_call x1, Pallas kernels, update_of(): pl.pallas_call(kernel, out_shape=jax.ShapeDtypeStruct((R0 + R1, PA), F32)...  88.6 us

profile of v2, /device:TPU:6, one launch (start us, length us, event | category | flops | bytes accessed | tf_op | source)
XLA Modules:
  0.0 91.7 jit_solution(438354198873166541)
XLA Ops:
  0.0 1.4 %copy.8.pair_ref = s32[16,2]{1,0:T(8,128)} copy(s32[16,2]{0,1:T(2,128)} %param.11) | data formatting | bytes 256 | tf_op args[4]
  1.4 88.6 %shard_map.73 = f32[11,2816]{1,0:T(8,128)} custom-call(s32[16]{0:T(128)} %kb_ref.1, s32[16,2]{1,0:T(8,128)} %copy.8.pair_ref, f32[32]{0:T(128)} %occ_ref.1, f32[16,176]{1,0:T(8,128)} %own_vir_ref.1, f32[16,176]{1,0:T(8,128)} %own_vir_ref.1, bf16[5632,176]{1,0:T(8,128)(2,1)} %bitcast.3, bf16[32,176,176]{2,1,0:T(8,128)(2,1)} %bitcast.4, ...), custom_call_target="tpu_custom_call" | custom-call | tf_op jit(solution)/shard_map/pallas_call | solution.py:322
  90.0 1.7 %reshape.15 = f32[1,11,16,176]{3,2,1,0:T(8,128)} reshape(f32[11,2816]{1,0:T(8,128)} %shard_map.73) | data formatting | bytes 247808 | tf_op jit(solution)/shard_map/reshape | solution.py:356

commit v3 on v2

--- a/solution.py
+++ b/solution.py
@@ -19,6 +19,7 @@
 KL = AUX * V
 PA = PAIRS * V
 HALF = PA // 2
+ROWS = PA // 4
 QP = 4
 R0, R1 = 8, 3
 N0, N1 = 16 * R0, 16 * R1
@@ -39,6 +40,14 @@
     y_peers = [(me, lax.rem(y + s, 4) * 4 + z) for s in (1, 2, 3)]
     z_peers = [(me, y * 4 + lax.rem(z + s, 4)) for s in (1, 2, 3)]
 
+    barrier = pltpu.get_barrier_semaphore()
+    for peer in y_peers + z_peers:
+        pl.semaphore_signal(barrier, inc=1, device_id=peer, device_id_type=MESH)
+
+    @pl.loop(1, SECTORS)
+    def _(s):
+        pl.semaphore_signal(barrier, inc=1, device_id=(lax.rem(me + s, SECTORS), vert), device_id_type=MESH)
+
     def r_in(g):
         return pltpu.make_async_copy(r_hbm.at[pl.ds(g * GROUP, GROUP)], r_v.at[pl.ds(g * GROUP, GROUP)], in_sem.at[g])
 
@@ -52,14 +61,6 @@
     t_in.start()
     for g in range(GROUPS):
         l_in(g).start()
-
-    barrier = pltpu.get_barrier_semaphore()
-    for peer in y_peers + z_peers:
-        pl.semaphore_signal(barrier, inc=1, device_id=peer, device_id_type=MESH)
-
-    @pl.loop(1, SECTORS)
-    def _(s):
-        pl.semaphore_signal(barrier, inc=1, device_id=(lax.rem(me + s, SECTORS), vert), device_id_type=MESH)
 
     mids = (mid_a, mid_b, mid_c)
 
@@ -147,11 +148,9 @@
         if g == 0:
             pl.semaphore_wait(barrier, SECTORS - 1 + 6)
         start_first(g)
-    for half in range(2):
-        start_first(GROUPS + half)
 
     pair_row = jnp.concatenate(
-        [jnp.full((1, V), occ_ref[pair_ref[p, 0]] + occ_ref[pair_ref[p, 1]], F32) for p in range(PAIRS)], axis=1
+        [jnp.full((1, V), occ_ref[pair_ref[0, p]] + occ_ref[pair_ref[1, p]], F32) for p in range(PAIRS)], axis=1
     )
     own_vir = own_vir_ref[pl.ds(me, 1), :]
     own_row = jnp.concatenate([own_vir] * PAIRS, axis=1)
@@ -182,121 +181,138 @@
         @pl.when(g == GROUPS // 2 - 1)
         def _():
             start_second(0)
+            for half in range(2):
+                start_first(GROUPS + half)
 
     start_second(1)
 
-    def add(acc, right, half):
-        lanes = pl.ds(half * 2 * GL, 2 * GL)
-
-        @pl.loop(0, 4)
-        def _(m):
-            rows = pl.ds(pl.multiple_of(m * (PA // 4), 16), PA // 4)
-            term = lax.dot_general(
-                h[rows, lanes], right[...], (((1,), (1,)), ((), ())), preferred_element_type=F32
-            )
-            acc[rows, :] = term if half == 0 else acc[rows, :] + term
-
-    def add0(half):
+    def product(rows, right, half):
+        return lax.dot_general(
+            h[rows, half * 2 * GL:(half + 1) * 2 * GL], right, (((1,), (1,)), ((), ())), preferred_element_type=F32
+        )
+
+    def wait0(half):
         for g in (2 * half, 2 * half + 1):
             part = recv0.at[:, pl.ds(g * GL, GL)]
             pltpu.make_async_copy(part, part, qr_sem.at[g]).wait()
-        add(acc0, recv0.at[:, pl.ds(half * 2 * GL, 2 * GL)], half)
-
-    def add1(half):
-        pltpu.make_async_copy(recv1.at[half], recv1.at[half], qr_sem.at[GROUPS + half]).wait()
-        add(acc1, recv1.at[half, :, pl.ds(0, 2 * GL)], half)
-
-    full1[...] = jnp.zeros_like(full1)
-    zsend1[...] = jnp.zeros_like(zsend1)
-    add0(0)
-    start_second(2)
-    add0(1)
 
     def y_copy(part, s):
-        src, dst = (ysend0, yrecv0) if part == 0 else (ysend1.at[part - 1], yrecv1.at[part - 1])
+        src, dst = (ysend0, yrecv0) if part < 2 else (ysend1, yrecv1)
         return pltpu.make_async_remote_copy(
-            src_ref=src.at[lax.rem(y + s, 4)], dst_ref=dst.at[s - 1],
+            src_ref=src.at[part % 2, lax.rem(y + s, 4)], dst_ref=dst.at[part % 2, s - 1],
             send_sem=ys_sem.at[part, s - 1], recv_sem=yr_sem.at[part, s - 1],
             device_id=y_peers[s - 1], device_id_type=MESH,
         )
 
     def z_copy(part, s):
-        src, dst = (zsend0, zrecv0) if part == 0 else (zsend1.at[part - 1], zrecv1.at[part - 1])
+        src, dst = (zsend0, zrecv0) if part < 2 else (zsend1, zrecv1)
         return pltpu.make_async_remote_copy(
-            src_ref=src.at[lax.rem(z + s, 4)], dst_ref=dst.at[s - 1],
+            src_ref=src.at[part % 2, lax.rem(z + s, 4)], dst_ref=dst.at[part % 2, s - 1],
             send_sem=zs_sem.at[part, s - 1], recv_sem=zr_sem.at[part, s - 1],
             device_id=z_peers[s - 1], device_id_type=MESH,
         )
 
-    @pl.loop(0, PA // 128)
-    def _(m):
-        at = pl.ds(pl.multiple_of(m * 128, 128), 128)
-        turned = acc0[at, :].T
-        full0[:, at] = turned
-        for j in range(4):
-            ysend0[j, :, at] = turned[32 * j:32 * (j + 1)].astype(BF16)
-
-    for s in (1, 2, 3):
-        y_copy(0, s).start()
-
-    add1(0)
-
-    for s in (1, 2, 3):
-        y_copy(0, s).wait()
-    total = full0[pl.ds(pl.multiple_of(32 * y, 8), 32), :]
-    for s in range(3):
-        total = total + yrecv0[s].astype(F32)
-    sum0[...] = total
-    for j in range(4):
-        part = sum0[8 * j:8 * (j + 1), :]
-        zsend0[j] = jnp.concatenate([part[:, :HALF], part[:, HALF:]], axis=0).astype(BF16)
-    for s in (1, 2, 3):
-        z_copy(0, s).start()
-
-    add1(1)
-
-    for part in (1, 2):
+    def y_send(part):
+        side = part % 2
+        acc = acc0 if part < 2 else acc1
+
         @pl.loop(0, HALF // 128)
         def _(m):
             at = pl.ds(pl.multiple_of(m * 128, 128), 128)
-            turned = acc1[pl.ds(pl.multiple_of((part - 1) * HALF + m * 128, 128), 128), :].T
-            for j in range(4):
-                full1[part - 1, j, 0:12, at] = turned[12 * j:12 * (j + 1)]
-
-        ysend1[part - 1] = full1[part - 1].astype(BF16)
+            turned = acc[pl.ds(pl.multiple_of(side * HALF + m * 128, 128), 128), :].T
+            if part < 2:
+                full0[side, :, at] = turned
+                for j in range(4):
+                    ysend0[side, j, :, at] = turned[32 * j:32 * (j + 1)].astype(BF16)
+            else:
+                for j in range(4):
+                    full1[side, j, 0:12, at] = turned[12 * j:12 * (j + 1)]
+
+        if part >= 2:
+            ysend1[side] = full1[side].astype(BF16)
         for s in (1, 2, 3):
             y_copy(part, s).start()
 
-    for s in (1, 2, 3):
-        z_copy(0, s).wait()
-    own = sum0[pl.ds(pl.multiple_of(8 * z, 8), 8), :]
-    low, high = own[:, :HALF], own[:, HALF:]
-    for s in range(3):
-        got = zrecv0[s].astype(F32)
-        low, high = low + got[0:8], high + got[8:16]
-    o_ref[0:8, :HALF] = low / den[0:8, :HALF]
-    o_ref[0:8, HALF:] = high / den[0:8, HALF:]
-
-    for part in (1, 2):
+    def z_send(part):
+        side = part % 2
         for s in (1, 2, 3):
             y_copy(part, s).wait()
-        rest = full1[part - 1, y]
-        for s in range(3):
-            rest = rest + yrecv1[part - 1, s].astype(F32)
-        for j in range(4):
-            zsend1[part - 1, j, 0:3, :] = rest[3 * j:3 * j + 3, :W2]
-            zsend1[part - 1, j, 4:7, :HALF - W2] = rest[3 * j:3 * j + 3, W2:]
+        if part < 2:
+            total = full0[side, pl.ds(pl.multiple_of(32 * y, 8), 32), :]
+            for s in range(3):
+                total = total + yrecv0[side, s].astype(F32)
+            sum0[side] = total
+            for j in range(4):
+                zsend0[side, j] = jnp.concatenate(
+                    [total[8 * j:8 * j + 8, :W2],
+                     jnp.concatenate([total[8 * j:8 * j + 8, W2:], jnp.zeros((8, 2 * W2 - HALF), F32)], axis=1)], axis=0
+                ).astype(BF16)
+        else:
+            total = full1[side, y]
+            for s in range(3):
+                total = total + yrecv1[side, s].astype(F32)
+            for j in range(4):
+                zsend1[side, j, 0:3, :] = total[3 * j:3 * j + 3, :W2]
+                zsend1[side, j, 4:7, :HALF - W2] = total[3 * j:3 * j + 3, W2:]
         for s in (1, 2, 3):
             z_copy(part, s).start()
-    for part in (1, 2):
+
+    def finish(part):
+        side = part % 2
+        at = side * HALF
         for s in (1, 2, 3):
             z_copy(part, s).wait()
-        last = zsend1[part - 1, z]
-        for s in range(3):
-            last = last + zrecv1[part - 1, s]
-        at = (part - 1) * HALF
-        o_ref[8:11, at:at + W2] = last[0:3] / den[8:11, at:at + W2]
-        o_ref[8:11, at + W2:at + HALF] = last[4:7, :HALF - W2] / den[8:11, at + W2:at + HALF]
+        if part < 2:
+            own = sum0[side, pl.ds(pl.multiple_of(8 * z, 8), 8), :]
+            low, high = own[:, :W2], own[:, W2:]
+            for s in range(3):
+                got = zrecv0[side, s].astype(F32)
+                low, high = low + got[0:8], high + got[8:16, :HALF - W2]
+            rows = pl.ds(0, R0)
+        else:
+            last = zsend1[side, z]
+            for s in range(3):
+                last = last + zrecv1[side, s]
+            low, high = last[0:R1], last[4:4 + R1, :HALF - W2]
+            rows = pl.ds(R0, R1)
+        o_ref[rows, at:at + W2] = low / den[rows, at:at + W2]
+        o_ref[rows, at + W2:at + HALF] = high / den[rows, at + W2:at + HALF]
+
+    full1[...] = jnp.zeros_like(full1)
+    zsend1[...] = jnp.zeros_like(zsend1)
+
+    wait0(0)
+
+    @pl.loop(0, 4)
+    def _(m):
+        rows = pl.ds(pl.multiple_of(m * ROWS, 16), ROWS)
+        acc0[rows, :] = product(rows, recv0[:, :2 * GL], 0)
+
+    start_second(2)
+    wait0(1)
+    for side in range(2):
+        @pl.loop(2 * side, 2 * side + 2)
+        def _(m):
+            rows = pl.ds(pl.multiple_of(m * ROWS, 16), ROWS)
+            acc0[rows, :] += product(rows, recv0[:, 2 * GL:], 1)
+
+        y_send(side)
+
+    for half in range(2):
+        pltpu.make_async_copy(recv1.at[half], recv1.at[half], qr_sem.at[GROUPS + half]).wait()
+    for side in range(2):
+        @pl.loop(2 * side, 2 * side + 2)
+        def _(m):
+            rows = pl.ds(pl.multiple_of(m * ROWS, 16), ROWS)
+            acc1[rows, :] = product(rows, recv1[0, :, :2 * GL], 0) + product(rows, recv1[1, :, :2 * GL], 1)
+
+        y_send(2 + side)
+        z_send(side)
+
+    z_send(2)
+    z_send(3)
+    for part in range(4):
+        finish(part)
 
     for unit in range(GROUPS + 2):
         @pl.when(core != unit % 2)
@@ -332,15 +348,15 @@
             vmem((2, SECTORS, 16, GL), BF16), vmem((SECTORS, N1, W1), BF16),
             vmem((N0, KL), BF16), vmem((2, N1, W1 * CHIPS), BF16), vmem((PA, KL), BF16),
             vmem((PA, N0), F32), vmem((PA, N1), F32), vmem((16, PA), F32),
-            vmem((N0, PA), F32), vmem((4, 32, PA), BF16), vmem((3, 32, PA), BF16),
-            vmem((32, PA), F32), vmem((4, 16, HALF), BF16), vmem((3, 16, HALF), BF16),
+            vmem((2, N0, HALF), F32), vmem((2, 4, 32, HALF), BF16), vmem((2, 3, 32, HALF), BF16),
+            vmem((2, 32, HALF), F32), vmem((2, 4, 16, W2), BF16), vmem((2, 3, 16, W2), BF16),
             vmem((2, 4, 16, HALF), F32), vmem((2, 4, 16, HALF), BF16), vmem((2, 3, 16, HALF), BF16),
             vmem((2, 4, 8, W2), F32), vmem((2, 3, 8, W2), F32),
             pltpu.SemaphoreType.DMA((2 * GROUPS + 1,)),
             pltpu.SemaphoreType.DMA((GROUPS + 2, CHIPS)), pltpu.SemaphoreType.DMA((3,)),
             pltpu.SemaphoreType.DMA((3, SECTORS)), pltpu.SemaphoreType.DMA((GROUPS + 2,)),
-            pltpu.SemaphoreType.DMA((3, 3)), pltpu.SemaphoreType.DMA((3, 3)),
-            pltpu.SemaphoreType.DMA((3, 3)), pltpu.SemaphoreType.DMA((3, 3)),
+            pltpu.SemaphoreType.DMA((4, 3)), pltpu.SemaphoreType.DMA((4, 3)),
+            pltpu.SemaphoreType.DMA((4, 3)), pltpu.SemaphoreType.DMA((4, 3)),
         ],
         compiler_params=pltpu.CompilerParams(
             collective_id=0, has_side_effects=True, vmem_limit_bytes=60 * 2**20
@@ -352,7 +368,7 @@
     left = left_factor.reshape(KL, V)
     right = right_factor.reshape(AUX, V, V)
     amps = amplitudes.reshape(PAIRS, V, V)
-    update = update_of(kb_table, pair_list, occ_energy, vir_energy, left, right, amps)
+    update = update_of(kb_table, pair_list.T, occ_energy, vir_energy, left, right, amps)
     return update.reshape(1, R0 + R1, PAIRS, V)
 
 

time: 91.9 us -> 84 us (0.914)
  Pallas kernels: 88.6 us -> 81.4 us
  local copies, waits for them, and re-layouts: 3.1 us -> 1.74 us
    pallas_call x1, Pallas kernels: 88.6 us -> 81.4 us  [update_of(): pl.pallas_call(kernel, out_shape=jax.ShapeDtypeStruct((R0 + R1, PA), F32)...]
    unnamed x1 -> x0, local copies, waits for them, and re-layouts: 1.35 us -> none
where the time goes in v3:
time: 84 us; the launch traced here: 83.2 us
  Pallas kernels  81.4 us (97%)
  local copies, waits for them, and re-layouts  1.74 us (2%)
    pallas_call x1, Pallas kernels, update_of(): pl.pallas_call(kernel, out_shape=jax.ShapeDtypeStruct((R0 + R1, PA), F32)...  81.4 us
    reshape x1, local copies, waits for them, and re-layouts, on_device(): return update.reshape(1, R0 + R1, PAIRS, V)  1.74 us

profile of v3, /device:TPU:6, one launch (start us, length us, event | category | flops | bytes accessed | tf_op | source)
XLA Modules:
  0.0 83.2 jit_solution(17466556614555448771)
XLA Ops:
  0.0 81.4 %shard_map.73 = f32[11,2816]{1,0:T(8,128)} custom-call(s32[16]{0:T(128)} %kb_ref.1, s32[2,16]{1,0:T(2,128)} %bitcast.7, f32[32]{0:T(128)} %occ_ref.1, f32[16,176]{1,0:T(8,128)} %own_vir_ref.1, f32[16,176]{1,0:T(8,128)} %own_vir_ref.1, bf16[5632,176]{1,0:T(8,128)(2,1)} %bitcast.4, bf16[32,176,176]{2,1,0:T(8,128)(2,1)} %bitcast.5, bf16[16,176,176]{2,1,0:T(8,128)(2,1)} %bitcast.6), custom_call_target="tpu_custom_call" | custom-call | tf_op jit(solution)/shard_map/pallas_call | solution.py:338
  81.4 1.7 %reshape.15 = f32[1,11,16,176]{3,2,1,0:T(8,128)} reshape(f32[11,2816]{1,0:T(8,128)} %shard_map.73) | data formatting | bytes 247808 | tf_op jit(solution)/shard_map/reshape | solution.py:372

commit v4 on v3

--- a/solution.py
+++ b/solution.py
@@ -18,20 +18,18 @@
 GL = GROUP * V
 KL = AUX * V
 PA = PAIRS * V
-HALF = PA // 2
-ROWS = PA // 4
+WIDE = (768, 640, 768, 640)
+FROM = (0, 768, 1408, 2176)
 QP = 4
 R0, R1 = 8, 3
 N0, N1 = 16 * R0, 16 * R1
 CHIPS = 8
-W2 = 768
 W1 = 384
 
 
 def kernel(kb_ref, pair_ref, occ_ref, vir_ref, own_vir_ref, l_hbm, r_hbm, t_hbm, o_ref,
-           l_v, r_v, t_v, t_cat, send0, send1, mid_a, mid_b, mid_c, out0, out1, recv0, recv1, h, acc0, acc1, den,
-           full0, ysend0, yrecv0, sum0, zsend0, zrecv0,
-           full1, ysend1, yrecv1, zsend1, zrecv1,
+           l_v, r_v, t_v, t_cat, send0, send1, mid_a, mid_b, mid_c, out0, out1, recv, h, acc, den,
+           full, ysend, yrecv, zsum, zsend, zrecv,
            in_sem, ps_sem, pr_sem, qs_sem, qr_sem, ys_sem, yr_sem, zs_sem, zr_sem):
     me = lax.axis_index("ka")
     vert = lax.axis_index("vert")
@@ -100,11 +98,11 @@
         if which < 2:
             src = out0.at[which, k]
             g = 2 * which + core
-            dst = recv0.at[pl.ds(pl.multiple_of(16 * chip, 16), 16), pl.ds(pl.multiple_of(g * GL, 128), GL)]
+            dst = recv.at[which, pl.ds(pl.multiple_of(16 * chip, 16), 16), pl.ds(pl.multiple_of(core * GL, 128), GL)]
         else:
             src = out1.at[k]
             g = GROUPS + core
-            dst = recv1.at[core, :, pl.ds(pl.multiple_of(W1 * chip, 128), W1)]
+            dst = recv.at[core, pl.ds(N0, N1), pl.ds(pl.multiple_of(W1 * chip, 128), W1)]
         return hop(src, dst, qs_sem.at[which, 2 * s + t], qr_sem.at[g], k, far)
 
     def start_first(unit):
@@ -147,7 +145,10 @@
         send1[g // 2, :, (g % 2) * GL:(g % 2 + 1) * GL] = packed[N0:]
         if g == 0:
             pl.semaphore_wait(barrier, SECTORS - 1 + 6)
-        start_first(g)
+        if g < 2:
+            start_first(g)
+    for unit in (GROUPS, GROUPS + 1, 2, 3):
+        start_first(unit)
 
     pair_row = jnp.concatenate(
         [jnp.full((1, V), occ_ref[pair_ref[0, p]] + occ_ref[pair_ref[1, p]], F32) for p in range(PAIRS)], axis=1
@@ -181,138 +182,99 @@
         @pl.when(g == GROUPS // 2 - 1)
         def _():
             start_second(0)
-            for half in range(2):
-                start_first(GROUPS + half)
+
+        @pl.when(g == GROUPS // 2)
+        def _():
+            start_second(2)
 
     start_second(1)
 
-    def product(rows, right, half):
+    def arrive(half):
+        for g in range(2):
+            part = recv.at[half, pl.ds(0, N0), pl.ds(g * GL, GL)]
+            pltpu.make_async_copy(part, part, qr_sem.at[2 * half + g]).wait()
+        part = recv.at[half, pl.ds(N0, N1), :]
+        pltpu.make_async_copy(part, part, qr_sem.at[GROUPS + half]).wait()
+
+    def product(rows, half):
         return lax.dot_general(
-            h[rows, half * 2 * GL:(half + 1) * 2 * GL], right, (((1,), (1,)), ((), ())), preferred_element_type=F32
+            h[rows, half * 2 * GL:(half + 1) * 2 * GL], recv[half, :, :2 * GL], (((1,), (1,)), ((), ())),
+            preferred_element_type=F32,
         )
 
-    def wait0(half):
-        for g in (2 * half, 2 * half + 1):
-            part = recv0.at[:, pl.ds(g * GL, GL)]
-            pltpu.make_async_copy(part, part, qr_sem.at[g]).wait()
-
     def y_copy(part, s):
-        src, dst = (ysend0, yrecv0) if part < 2 else (ysend1, yrecv1)
         return pltpu.make_async_remote_copy(
-            src_ref=src.at[part % 2, lax.rem(y + s, 4)], dst_ref=dst.at[part % 2, s - 1],
+            src_ref=ysend.at[part, lax.rem(y + s, 4), :, pl.ds(0, WIDE[part])],
+            dst_ref=yrecv.at[part, s - 1, :, pl.ds(0, WIDE[part])],
             send_sem=ys_sem.at[part, s - 1], recv_sem=yr_sem.at[part, s - 1],
             device_id=y_peers[s - 1], device_id_type=MESH,
         )
 
     def z_copy(part, s):
-        src, dst = (zsend0, zrecv0) if part < 2 else (zsend1, zrecv1)
         return pltpu.make_async_remote_copy(
-            src_ref=src.at[part % 2, lax.rem(z + s, 4)], dst_ref=dst.at[part % 2, s - 1],
+            src_ref=zsend.at[part, lax.rem(z + s, 4), :, pl.ds(0, WIDE[part])],
+            dst_ref=zrecv.at[part, s - 1, :, pl.ds(0, WIDE[part])],
             send_sem=zs_sem.at[part, s - 1], recv_sem=zr_sem.at[part, s - 1],
             device_id=z_peers[s - 1], device_id_type=MESH,
         )
 
     def y_send(part):
-        side = part % 2
-        acc = acc0 if part < 2 else acc1
-
-        @pl.loop(0, HALF // 128)
-        def _(m):
-            at = pl.ds(pl.multiple_of(m * 128, 128), 128)
-            turned = acc[pl.ds(pl.multiple_of(side * HALF + m * 128, 128), 128), :].T
-            if part < 2:
-                full0[side, :, at] = turned
-                for j in range(4):
-                    ysend0[side, j, :, at] = turned[32 * j:32 * (j + 1)].astype(BF16)
-            else:
-                for j in range(4):
-                    full1[side, j, 0:12, at] = turned[12 * j:12 * (j + 1)]
-
-        if part >= 2:
-            ysend1[side] = full1[side].astype(BF16)
+        for m in range(WIDE[part] // 128):
+            at = slice(m * 128, (m + 1) * 128)
+            rows = slice(FROM[part] + m * 128, FROM[part] + (m + 1) * 128)
+            early, late = acc[rows, :N0].T, acc[rows, N0:].T
+            for j in range(4):
+                full[part, j, 0:32, at] = early[32 * j:32 * (j + 1)]
+                full[part, j, 32:44, at] = late[12 * j:12 * (j + 1)]
+        for j in range(4):
+            ysend[part, j] = full[part, j].astype(BF16)
         for s in (1, 2, 3):
             y_copy(part, s).start()
 
     def z_send(part):
-        side = part % 2
+        w = WIDE[part]
         for s in (1, 2, 3):
             y_copy(part, s).wait()
-        if part < 2:
-            total = full0[side, pl.ds(pl.multiple_of(32 * y, 8), 32), :]
-            for s in range(3):
-                total = total + yrecv0[side, s].astype(F32)
-            sum0[side] = total
-            for j in range(4):
-                zsend0[side, j] = jnp.concatenate(
-                    [total[8 * j:8 * j + 8, :W2],
-                     jnp.concatenate([total[8 * j:8 * j + 8, W2:], jnp.zeros((8, 2 * W2 - HALF), F32)], axis=1)], axis=0
-                ).astype(BF16)
-        else:
-            total = full1[side, y]
-            for s in range(3):
-                total = total + yrecv1[side, s].astype(F32)
-            for j in range(4):
-                zsend1[side, j, 0:3, :] = total[3 * j:3 * j + 3, :W2]
-                zsend1[side, j, 4:7, :HALF - W2] = total[3 * j:3 * j + 3, W2:]
+        total = full[part, y, :, :w]
+        for s in range(3):
+            total = total + yrecv[part, s, :, :w].astype(F32)
+        for j in range(4):
+            zsum[part, j, 0:8, :w] = total[8 * j:8 * j + 8]
+            zsum[part, j, 8:11, :w] = total[32 + 3 * j:35 + 3 * j]
+        for j in range(4):
+            zsend[part, j] = zsum[part, j].astype(BF16)
         for s in (1, 2, 3):
             z_copy(part, s).start()
 
     def finish(part):
-        side = part % 2
-        at = side * HALF
+        w, at = WIDE[part], FROM[part]
         for s in (1, 2, 3):
             z_copy(part, s).wait()
-        if part < 2:
-            own = sum0[side, pl.ds(pl.multiple_of(8 * z, 8), 8), :]
-            low, high = own[:, :W2], own[:, W2:]
-            for s in range(3):
-                got = zrecv0[side, s].astype(F32)
-                low, high = low + got[0:8], high + got[8:16, :HALF - W2]
-            rows = pl.ds(0, R0)
-        else:
-            last = zsend1[side, z]
-            for s in range(3):
-                last = last + zrecv1[side, s]
-            low, high = last[0:R1], last[4:4 + R1, :HALF - W2]
-            rows = pl.ds(R0, R1)
-        o_ref[rows, at:at + W2] = low / den[rows, at:at + W2]
-        o_ref[rows, at + W2:at + HALF] = high / den[rows, at + W2:at + HALF]
-
-    full1[...] = jnp.zeros_like(full1)
-    zsend1[...] = jnp.zeros_like(zsend1)
-
-    wait0(0)
+        total = zsum[part, z, :, :w]
+        for s in range(3):
+            total = total + zrecv[part, s, :, :w].astype(F32)
+        o_ref[:, at:at + w] = total[:R0 + R1] / den[:R0 + R1, at:at + w]
+
+    full[...] = jnp.zeros_like(full)
+    zsum[...] = jnp.zeros_like(zsum)
+
+    arrive(0)
 
     @pl.loop(0, 4)
     def _(m):
-        rows = pl.ds(pl.multiple_of(m * ROWS, 16), ROWS)
-        acc0[rows, :] = product(rows, recv0[:, :2 * GL], 0)
-
-    start_second(2)
-    wait0(1)
-    for side in range(2):
-        @pl.loop(2 * side, 2 * side + 2)
-        def _(m):
-            rows = pl.ds(pl.multiple_of(m * ROWS, 16), ROWS)
-            acc0[rows, :] += product(rows, recv0[:, 2 * GL:], 1)
-
-        y_send(side)
-
-    for half in range(2):
-        pltpu.make_async_copy(recv1.at[half], recv1.at[half], qr_sem.at[GROUPS + half]).wait()
-    for side in range(2):
-        @pl.loop(2 * side, 2 * side + 2)
-        def _(m):
-            rows = pl.ds(pl.multiple_of(m * ROWS, 16), ROWS)
-            acc1[rows, :] = product(rows, recv1[0, :, :2 * GL], 0) + product(rows, recv1[1, :, :2 * GL], 1)
-
-        y_send(2 + side)
-        z_send(side)
-
-    z_send(2)
-    z_send(3)
+        rows = pl.ds(pl.multiple_of(m * (PA // 4), 16), PA // 4)
+        acc[rows, :] = product(rows, 0)
+
+    arrive(1)
     for part in range(4):
-        finish(part)
+        rows = slice(FROM[part], FROM[part] + WIDE[part])
+        acc[rows, :] += product(rows, 1)
+        y_send(part)
+    for part in range(4):
+        z_send(part)
+        if part > 0:
+            finish(part - 1)
+    finish(3)
 
     for unit in range(GROUPS + 2):
         @pl.when(core != unit % 2)
@@ -346,12 +308,9 @@
             vmem((N0, KL), BF16), vmem((2, N1, W1 * CHIPS), BF16),
             vmem((SECTORS, 16, GL), BF16), vmem((SECTORS, 16, GL), BF16), vmem((SECTORS, N1, W1), BF16),
             vmem((2, SECTORS, 16, GL), BF16), vmem((SECTORS, N1, W1), BF16),
-            vmem((N0, KL), BF16), vmem((2, N1, W1 * CHIPS), BF16), vmem((PA, KL), BF16),
-            vmem((PA, N0), F32), vmem((PA, N1), F32), vmem((16, PA), F32),
-            vmem((2, N0, HALF), F32), vmem((2, 4, 32, HALF), BF16), vmem((2, 3, 32, HALF), BF16),
-            vmem((2, 32, HALF), F32), vmem((2, 4, 16, W2), BF16), vmem((2, 3, 16, W2), BF16),
-            vmem((2, 4, 16, HALF), F32), vmem((2, 4, 16, HALF), BF16), vmem((2, 3, 16, HALF), BF16),
-            vmem((2, 4, 8, W2), F32), vmem((2, 3, 8, W2), F32),
+            vmem((2, V, W1 * CHIPS), BF16), vmem((PA, KL), BF16), vmem((PA, V), F32), vmem((16, PA), F32),
+            vmem((4, 4, 48, 768), F32), vmem((4, 4, 48, 768), BF16), vmem((4, 3, 48, 768), BF16),
+            vmem((4, 4, 16, 768), F32), vmem((4, 4, 16, 768), BF16), vmem((4, 3, 16, 768), BF16),
             pltpu.SemaphoreType.DMA((2 * GROUPS + 1,)),
             pltpu.SemaphoreType.DMA((GROUPS + 2, CHIPS)), pltpu.SemaphoreType.DMA((3,)),
             pltpu.SemaphoreType.DMA((3, SECTORS)), pltpu.SemaphoreType.DMA((GROUPS + 2,)),

time: 84 us -> 84.2 us (level)
  Pallas kernels: 81.4 us -> 82.3 us
    pallas_call x1, Pallas kernels: 81.4 us -> 82.3 us  [update_of(): pl.pallas_call(kernel, out_shape=jax.ShapeDtypeStruct((R0 + R1, PA), F32)...]
where the time goes in v4:
time: 84.2 us; the launch traced here: 84.1 us
  Pallas kernels  82.3 us (98%)
  local copies, waits for them, and re-layouts  1.74 us (2%)
    pallas_call x1, Pallas kernels, update_of(): pl.pallas_call(kernel, out_shape=jax.ShapeDtypeStruct((R0 + R1, PA), F32)...  82.3 us
    reshape x1, local copies, waits for them, and re-layouts, on_device(): return update.reshape(1, R0 + R1, PAIRS, V)  1.74 us

profile of v4, /device:TPU:6, one launch (start us, length us, event | category | flops | bytes accessed | tf_op | source)
XLA Modules:
  0.0 84.1 jit_solution(12363098004137644212)
XLA Ops:
  0.0 82.3 %shard_map.73 = f32[11,2816]{1,0:T(8,128)} custom-call(s32[16]{0:T(128)} %kb_ref.1, s32[2,16]{1,0:T(2,128)} %bitcast.7, f32[32]{0:T(128)} %occ_ref.1, f32[16,176]{1,0:T(8,128)} %own_vir_ref.1, f32[16,176]{1,0:T(8,128)} %own_vir_ref.1, bf16[5632,176]{1,0:T(8,128)(2,1)} %bitcast.4, bf16[32,176,176]{2,1,0:T(8,128)(2,1)} %bitcast.5, bf16[16,176,176]{2,1,0:T(8,128)(2,1)} %bitcast.6), custom_call_target="tpu_custom_call" | custom-call | tf_op jit(solution)/shard_map/pallas_call | solution.py:300
  82.3 1.7 %reshape.15 = f32[1,11,16,176]{3,2,1,0:T(8,128)} reshape(f32[11,2816]{1,0:T(8,128)} %shard_map.73) | data formatting | bytes 247808 | tf_op jit(solution)/shard_map/reshape | solution.py:331

commit v5 on v4

--- a/solution.py
+++ b/solution.py
@@ -18,8 +18,9 @@
 GL = GROUP * V
 KL = AUX * V
 PA = PAIRS * V
-WIDE = (768, 640, 768, 640)
-FROM = (0, 768, 1408, 2176)
+WIDE = (896, 896, 640, 384)
+FROM = (0, 896, 1792, 2432)
+ZWIDE = (896, 640, 896)
 QP = 4
 R0, R1 = 8, 3
 N0, N1 = 16 * R0, 16 * R1
@@ -28,7 +29,7 @@
 
 
 def kernel(kb_ref, pair_ref, occ_ref, vir_ref, own_vir_ref, l_hbm, r_hbm, t_hbm, o_ref,
-           l_v, r_v, t_v, t_cat, send0, send1, mid_a, mid_b, mid_c, out0, out1, recv, h, acc, den,
+           l_v, r_v, t_v, t_cat, send0, send1, mid_a, mid_b, mid_c, out0, out1, recv, h, acc_f, acc_l, den,
            full, ysend, yrecv, zsum, zsend, zrecv,
            in_sem, ps_sem, pr_sem, qs_sem, qr_sem, ys_sem, yr_sem, zs_sem, zr_sem):
     me = lax.axis_index("ka")
@@ -38,14 +39,6 @@
     y_peers = [(me, lax.rem(y + s, 4) * 4 + z) for s in (1, 2, 3)]
     z_peers = [(me, y * 4 + lax.rem(z + s, 4)) for s in (1, 2, 3)]
 
-    barrier = pltpu.get_barrier_semaphore()
-    for peer in y_peers + z_peers:
-        pl.semaphore_signal(barrier, inc=1, device_id=peer, device_id_type=MESH)
-
-    @pl.loop(1, SECTORS)
-    def _(s):
-        pl.semaphore_signal(barrier, inc=1, device_id=(lax.rem(me + s, SECTORS), vert), device_id_type=MESH)
-
     def r_in(g):
         return pltpu.make_async_copy(r_hbm.at[pl.ds(g * GROUP, GROUP)], r_v.at[pl.ds(g * GROUP, GROUP)], in_sem.at[g])
 
@@ -60,13 +53,25 @@
     for g in range(GROUPS):
         l_in(g).start()
 
+    barrier = pltpu.get_barrier_semaphore()
+    for peer in y_peers + z_peers:
+        pl.semaphore_signal(barrier, inc=1, device_id=peer, device_id_type=MESH)
+
+    @pl.loop(1, SECTORS)
+    def _(s):
+        pl.semaphore_signal(barrier, inc=1, device_id=(lax.rem(me + s, SECTORS), vert), device_id_type=MESH)
+
     mids = (mid_a, mid_b, mid_c)
 
     row = lax.broadcasted_iota(jnp.int32, (V, V), 0)
     col = lax.broadcasted_iota(jnp.int32, (V, V), 1)
     late = row - N0
     third = lax.shift_right_logical(late * 21846, 16)
-    source = jnp.where(row < N0, 11 * lax.shift_right_logical(row, 3) + (row & 7), 11 * third + R0 + (late - 3 * third))
+    source = jnp.where(
+        row < N0,
+        11 * lax.shift_right_logical(row & 63, 2) + (row & 3) + 4 * lax.shift_right_logical(row, 6),
+        11 * third + R0 + (late - 3 * third),
+    )
     order = (col == source).astype(F32).astype(BF16)
 
     for half in range(2):
@@ -83,7 +88,8 @@
     def first(unit, s, far):
         j = lax.rem(chip + s, CHIPS)
         if unit < GROUPS:
-            src = send0.at[pl.ds(pl.multiple_of(16 * j, 16), 16), pl.ds(unit * GL, GL)]
+            g = 2 * (unit % 2) + j // 4
+            src = send0.at[pl.ds(pl.multiple_of(64 * (unit // 2) + 16 * lax.rem(j, 4), 16), 16), pl.ds(pl.multiple_of(g * GL, 128), GL)]
             dst = mids[unit // 2].at[me]
             which = unit // 2
         else:
@@ -98,7 +104,8 @@
         if which < 2:
             src = out0.at[which, k]
             g = 2 * which + core
-            dst = recv.at[which, pl.ds(pl.multiple_of(16 * chip, 16), 16), pl.ds(pl.multiple_of(core * GL, 128), GL)]
+            rows = pl.ds(pl.multiple_of(64 * which + 16 * lax.rem(chip, 4), 16), 16)
+            dst = recv.at[core, rows, pl.ds(pl.multiple_of(chip // 4 * GL, 128), GL)]
         else:
             src = out1.at[k]
             g = GROUPS + core
@@ -145,8 +152,8 @@
         send1[g // 2, :, (g % 2) * GL:(g % 2 + 1) * GL] = packed[N0:]
         if g == 0:
             pl.semaphore_wait(barrier, SECTORS - 1 + 6)
-        if g < 2:
-            start_first(g)
+        if g % 2 == 1:
+            start_first(g // 2)
     for unit in (GROUPS, GROUPS + 1, 2, 3):
         start_first(unit)
 
@@ -189,101 +196,16 @@
 
     start_second(1)
 
-    def arrive(half):
-        for g in range(2):
-            part = recv.at[half, pl.ds(0, N0), pl.ds(g * GL, GL)]
-            pltpu.make_async_copy(part, part, qr_sem.at[2 * half + g]).wait()
-        part = recv.at[half, pl.ds(N0, N1), :]
-        pltpu.make_async_copy(part, part, qr_sem.at[GROUPS + half]).wait()
-
-    def product(rows, half):
-        return lax.dot_general(
-            h[rows, half * 2 * GL:(half + 1) * 2 * GL], recv[half, :, :2 * GL], (((1,), (1,)), ((), ())),
-            preferred_element_type=F32,
-        )
-
-    def y_copy(part, s):
-        return pltpu.make_async_remote_copy(
-            src_ref=ysend.at[part, lax.rem(y + s, 4), :, pl.ds(0, WIDE[part])],
-            dst_ref=yrecv.at[part, s - 1, :, pl.ds(0, WIDE[part])],
-            send_sem=ys_sem.at[part, s - 1], recv_sem=yr_sem.at[part, s - 1],
-            device_id=y_peers[s - 1], device_id_type=MESH,
-        )
-
-    def z_copy(part, s):
-        return pltpu.make_async_remote_copy(
-            src_ref=zsend.at[part, lax.rem(z + s, 4), :, pl.ds(0, WIDE[part])],
-            dst_ref=zrecv.at[part, s - 1, :, pl.ds(0, WIDE[part])],
-            send_sem=zs_sem.at[part, s - 1], recv_sem=zr_sem.at[part, s - 1],
-            device_id=z_peers[s - 1], device_id_type=MESH,
-        )
-
-    def y_send(part):
-        for m in range(WIDE[part] // 128):
-            at = slice(m * 128, (m + 1) * 128)
-            rows = slice(FROM[part] + m * 128, FROM[part] + (m + 1) * 128)
-            early, late = acc[rows, :N0].T, acc[rows, N0:].T
-            for j in range(4):
-                full[part, j, 0:32, at] = early[32 * j:32 * (j + 1)]
-                full[part, j, 32:44, at] = late[12 * j:12 * (j + 1)]
-        for j in range(4):
-            ysend[part, j] = full[part, j].astype(BF16)
-        for s in (1, 2, 3):
-            y_copy(part, s).start()
-
-    def z_send(part):
-        w = WIDE[part]
-        for s in (1, 2, 3):
-            y_copy(part, s).wait()
-        total = full[part, y, :, :w]
-        for s in range(3):
-            total = total + yrecv[part, s, :, :w].astype(F32)
-        for j in range(4):
-            zsum[part, j, 0:8, :w] = total[8 * j:8 * j + 8]
-            zsum[part, j, 8:11, :w] = total[32 + 3 * j:35 + 3 * j]
-        for j in range(4):
-            zsend[part, j] = zsum[part, j].astype(BF16)
-        for s in (1, 2, 3):
-            z_copy(part, s).start()
-
-    def finish(part):
-        w, at = WIDE[part], FROM[part]
-        for s in (1, 2, 3):
-            z_copy(part, s).wait()
-        total = zsum[part, z, :, :w]
-        for s in range(3):
-            total = total + zrecv[part, s, :, :w].astype(F32)
-        o_ref[:, at:at + w] = total[:R0 + R1] / den[:R0 + R1, at:at + w]
-
-    full[...] = jnp.zeros_like(full)
-    zsum[...] = jnp.zeros_like(zsum)
-
-    arrive(0)
-
-    @pl.loop(0, 4)
-    def _(m):
-        rows = pl.ds(pl.multiple_of(m * (PA // 4), 16), PA // 4)
-        acc[rows, :] = product(rows, 0)
-
-    arrive(1)
-    for part in range(4):
-        rows = slice(FROM[part], FROM[part] + WIDE[part])
-        acc[rows, :] += product(rows, 1)
-        y_send(part)
-    for part in range(4):
-        z_send(part)
-        if part > 0:
-            finish(part - 1)
-    finish(3)
-
-    for unit in range(GROUPS + 2):
-        @pl.when(core != unit % 2)
-        def _():
-            first(unit, 0, True).wait_send()
-
-        for s in range(1, CHIPS):
-            first(unit, s, True).wait_send()
-    for which in range(3):
+    def sent_first():
+        for unit in range(GROUPS + 2):
+            @pl.when(core != unit % 2)
+            def _():
+                first(unit, 0, True).wait_send()
+
+            for s in range(1, CHIPS):
+                first(unit, s, True).wait_send()
+
+    def sent_second(which):
         for t in range(2):
             @pl.when(core != t)
             def _():
@@ -291,6 +213,134 @@
 
             for s in range(1, CHIPS):
                 second(which, s, t, True).wait_send()
+
+    def arrive(unit, rows, lanes):
+        for half in range(2):
+            part = recv.at[half, rows, lanes]
+            pltpu.make_async_copy(part, part, qr_sem.at[unit + half]).wait()
+
+    def product(rows, b_from, b_to):
+        terms = [
+            lax.dot_general(
+                h[rows, half * 2 * GL:(half + 1) * 2 * GL], recv[half, b_from:b_to, :2 * GL], (((1,), (1,)), ((), ())),
+                preferred_element_type=F32,
+            )
+            for half in range(2)
+        ]
+        return terms[0] + terms[1]
+
+    def y_copy(part, s, last):
+        rows = pl.ds(16, 32) if last else pl.ds(0, 16)
+        return pltpu.make_async_remote_copy(
+            src_ref=ysend.at[part, lax.rem(y + s, 4), rows, pl.ds(0, WIDE[part])],
+            dst_ref=yrecv.at[part, s - 1, rows, pl.ds(0, WIDE[part])],
+            send_sem=ys_sem.at[last, part, s - 1], recv_sem=yr_sem.at[last, part, s - 1],
+            device_id=y_peers[s - 1], device_id_type=MESH,
+        )
+
+    def z_copy(pack, s):
+        return pltpu.make_async_remote_copy(
+            src_ref=zsend.at[pack, lax.rem(z + s, 4), :, pl.ds(0, ZWIDE[pack])],
+            dst_ref=zrecv.at[pack, s - 1, :, pl.ds(0, ZWIDE[pack])],
+            send_sem=zs_sem.at[pack, s - 1], recv_sem=zr_sem.at[pack, s - 1],
+            device_id=z_peers[s - 1], device_id_type=MESH,
+        )
+
+    def y_send(part, last):
+        @pl.loop(0, WIDE[part] // 128)
+        def _(m):
+            at = pl.ds(pl.multiple_of(m * 128, 128), 128)
+            rows = pl.ds(pl.multiple_of(FROM[part] + m * 128, 128), 128)
+            if last:
+                turned = acc_l[rows, :].T
+                for j in range(4):
+                    full[part, j, 16:32, at] = turned[16 * j:16 * (j + 1)]
+                    full[part, j, 32:44, at] = turned[64 + 12 * j:64 + 12 * (j + 1)]
+            else:
+                turned = acc_f[rows, :].T
+                for j in range(4):
+                    full[part, j, 0:16, at] = turned[16 * j:16 * (j + 1)]
+
+        own = slice(16, 48) if last else slice(0, 16)
+        for j in range(4):
+            ysend[part, j, own] = full[part, j, own].astype(BF16)
+        for s in (1, 2, 3):
+            y_copy(part, s, last).start()
+
+    def y_sum(part, last):
+        w = WIDE[part]
+        rows = slice(16, 48) if last else slice(0, 16)
+        for s in (1, 2, 3):
+            y_copy(part, s, last).wait()
+        total = full[part, y, rows, :w]
+        for s in range(3):
+            total = total + yrecv[part, s, rows, :w].astype(F32)
+        for j in range(4):
+            if last:
+                at = 8 * (part % 2)
+                zsum[part // 2, j, at:at + 4, :w] = total[4 * j:4 * j + 4]
+                zsum[part // 2, j, at + 4:at + 7, :w] = total[16 + 3 * j:19 + 3 * j]
+            else:
+                zsum[2, j, 4 * part:4 * part + 4, :w] = total[4 * j:4 * j + 4]
+
+    def z_send(pack):
+        for j in range(4):
+            zsend[pack, j] = zsum[pack, j].astype(BF16)
+        for s in (1, 2, 3):
+            z_copy(pack, s).start()
+
+    def finish(pack):
+        for s in (1, 2, 3):
+            z_copy(pack, s).wait()
+        total = zsum[pack, z, :, :ZWIDE[pack]]
+        for s in range(3):
+            total = total + zrecv[pack, s, :, :ZWIDE[pack]].astype(F32)
+        for part in ((2 * pack, 2 * pack + 1) if pack < 2 else range(4)):
+            w, at = WIDE[part], FROM[part]
+            if pack < 2:
+                o_ref[4:11, at:at + w] = total[8 * (part % 2):8 * (part % 2) + 7, :w] / den[4:11, at:at + w]
+            else:
+                o_ref[0:4, at:at + w] = total[4 * part:4 * part + 4, :w] / den[0:4, at:at + w]
+
+    full[...] = jnp.zeros_like(full)
+    zsum[...] = jnp.zeros_like(zsum)
+
+    sent_first()
+    arrive(0, pl.ds(0, 64), pl.ds(0, 2 * GL))
+
+    @pl.loop(0, 4)
+    def _(m):
+        rows = pl.ds(pl.multiple_of(m * (PA // 4), 16), PA // 4)
+        acc_f[rows, :] = product(rows, 0, 64)
+
+    for part in range(4):
+        y_send(part, 0)
+    sent_second(0)
+    arrive(GROUPS, pl.ds(N0, N1), slice(None))
+    sent_second(2)
+    arrive(2, pl.ds(64, 64), pl.ds(0, 2 * GL))
+    for part in range(4):
+        @pl.loop(0, 2)
+        def _(m):
+            rows = pl.ds(pl.multiple_of(FROM[part] + m * (WIDE[part] // 2), 64), WIDE[part] // 2)
+            acc_l[rows, :] = product(rows, 64, V)
+
+        y_send(part, 1)
+        if part == 1:
+            for first_part in range(4):
+                y_sum(first_part, 0)
+            z_send(2)
+        if part == 2:
+            for early_part in range(2):
+                y_sum(early_part, 1)
+            z_send(0)
+    sent_second(1)
+    finish(2)
+    y_sum(2, 1)
+    y_sum(3, 1)
+    z_send(1)
+    finish(0)
+    finish(1)
 
 
 def update_of(kb_table, pair_list, occ_energy, vir_energy, left, right, amps):
@@ -308,14 +358,15 @@
             vmem((N0, KL), BF16), vmem((2, N1, W1 * CHIPS), BF16),
             vmem((SECTORS, 16, GL), BF16), vmem((SECTORS, 16, GL), BF16), vmem((SECTORS, N1, W1), BF16),
             vmem((2, SECTORS, 16, GL), BF16), vmem((SECTORS, N1, W1), BF16),
-            vmem((2, V, W1 * CHIPS), BF16), vmem((PA, KL), BF16), vmem((PA, V), F32), vmem((16, PA), F32),
-            vmem((4, 4, 48, 768), F32), vmem((4, 4, 48, 768), BF16), vmem((4, 3, 48, 768), BF16),
-            vmem((4, 4, 16, 768), F32), vmem((4, 4, 16, 768), BF16), vmem((4, 3, 16, 768), BF16),
+            vmem((2, V, W1 * CHIPS), BF16), vmem((PA, KL), BF16), vmem((PA, 64), F32), vmem((PA, V - 64), F32),
+            vmem((16, PA), F32),
+            vmem((4, 4, 48, 896), F32), vmem((4, 4, 48, 896), BF16), vmem((4, 3, 48, 896), BF16),
+            vmem((3, 4, 16, 896), F32), vmem((3, 4, 16, 896), BF16), vmem((3, 3, 16, 896), BF16),
             pltpu.SemaphoreType.DMA((2 * GROUPS + 1,)),
             pltpu.SemaphoreType.DMA((GROUPS + 2, CHIPS)), pltpu.SemaphoreType.DMA((3,)),
             pltpu.SemaphoreType.DMA((3, SECTORS)), pltpu.SemaphoreType.DMA((GROUPS + 2,)),
-            pltpu.SemaphoreType.DMA((4, 3)), pltpu.SemaphoreType.DMA((4, 3)),
-            pltpu.SemaphoreType.DMA((4, 3)), pltpu.SemaphoreType.DMA((4, 3)),
+            pltpu.SemaphoreType.DMA((2, 4, 3)), pltpu.SemaphoreType.DMA((2, 4, 3)),
+            pltpu.SemaphoreType.DMA((3, 3)), pltpu.SemaphoreType.DMA((3, 3)),
         ],
         compiler_params=pltpu.CompilerParams(
             collective_id=0, has_side_effects=True, vmem_limit_bytes=60 * 2**20

time: 84.2 us -> 84.8 us (level)
  no operation moved by 1% of the time
where the time goes in v5:
time: 84.8 us; the launch traced here: 84.6 us
  Pallas kernels  82.8 us (98%)
  local copies, waits for them, and re-layouts  1.74 us (2%)
    pallas_call x1, Pallas kernels, update_of(): pl.pallas_call(kernel, out_shape=jax.ShapeDtypeStruct((R0 + R1, PA), F32)...  82.8 us
    reshape x1, local copies, waits for them, and re-layouts, on_device(): return update.reshape(1, R0 + R1, PAIRS, V)  1.74 us

profile of v5, /device:TPU:6, one launch (start us, length us, event | category | flops | bytes accessed | tf_op | source)
XLA Modules:
  0.0 84.6 jit_solution(6677556793955616693)
XLA Ops:
  0.0 82.8 %shard_map.73 = f32[11,2816]{1,0:T(8,128)} custom-call(s32[16]{0:T(128)} %kb_ref.1, s32[2,16]{1,0:T(2,128)} %bitcast.7, f32[32]{0:T(128)} %occ_ref.1, f32[16,176]{1,0:T(8,128)} %own_vir_ref.1, f32[16,176]{1,0:T(8,128)} %own_vir_ref.1, bf16[5632,176]{1,0:T(8,128)(2,1)} %bitcast.4, bf16[32,176,176]{2,1,0:T(8,128)(2,1)} %bitcast.5, bf16[16,176,176]{2,1,0:T(8,128)(2,1)} %bitcast.6), custom_call_target="tpu_custom_call" | custom-call | tf_op jit(solution)/shard_map/pallas_call | solution.py:350
  82.9 1.7 %reshape.15 = f32[1,11,16,176]{3,2,1,0:T(8,128)} reshape(f32[11,2816]{1,0:T(8,128)} %shard_map.73) | data formatting | bytes 247808 | tf_op jit(solution)/shard_map/reshape | solution.py:382

commit v6 on v4

--- a/solution.py
+++ b/solution.py
@@ -18,8 +18,8 @@
 GL = GROUP * V
 KL = AUX * V
 PA = PAIRS * V
-WIDE = (768, 640, 768, 640)
-FROM = (0, 768, 1408, 2176)
+WIDE = (512, 896, 896, 512)
+FROM = (0, 512, 1408, 2304)
 QP = 4
 R0, R1 = 8, 3
 N0, N1 = 16 * R0, 16 * R1
@@ -38,14 +38,6 @@
     y_peers = [(me, lax.rem(y + s, 4) * 4 + z) for s in (1, 2, 3)]
     z_peers = [(me, y * 4 + lax.rem(z + s, 4)) for s in (1, 2, 3)]
 
-    barrier = pltpu.get_barrier_semaphore()
-    for peer in y_peers + z_peers:
-        pl.semaphore_signal(barrier, inc=1, device_id=peer, device_id_type=MESH)
-
-    @pl.loop(1, SECTORS)
-    def _(s):
-        pl.semaphore_signal(barrier, inc=1, device_id=(lax.rem(me + s, SECTORS), vert), device_id_type=MESH)
-
     def r_in(g):
         return pltpu.make_async_copy(r_hbm.at[pl.ds(g * GROUP, GROUP)], r_v.at[pl.ds(g * GROUP, GROUP)], in_sem.at[g])
 
@@ -59,6 +51,14 @@
     t_in.start()
     for g in range(GROUPS):
         l_in(g).start()
+
+    barrier = pltpu.get_barrier_semaphore()
+    for peer in y_peers + z_peers:
+        pl.semaphore_signal(barrier, inc=1, device_id=peer, device_id_type=MESH)
+
+    @pl.loop(1, SECTORS)
+    def _(s):
+        pl.semaphore_signal(barrier, inc=1, device_id=(lax.rem(me + s, SECTORS), vert), device_id_type=MESH)
 
     mids = (mid_a, mid_b, mid_c)
 
@@ -219,9 +219,10 @@
         )
 
     def y_send(part):
-        for m in range(WIDE[part] // 128):
-            at = slice(m * 128, (m + 1) * 128)
-            rows = slice(FROM[part] + m * 128, FROM[part] + (m + 1) * 128)
+        @pl.loop(0, WIDE[part] // 128)
+        def _(m):
+            at = pl.ds(pl.multiple_of(m * 128, 128), 128)
+            rows = pl.ds(pl.multiple_of(FROM[part] + m * 128, 128), 128)
             early, late = acc[rows, :N0].T, acc[rows, N0:].T
             for j in range(4):
                 full[part, j, 0:32, at] = early[32 * j:32 * (j + 1)]
@@ -267,13 +268,17 @@
 
     arrive(1)
     for part in range(4):
-        rows = slice(FROM[part], FROM[part] + WIDE[part])
-        acc[rows, :] += product(rows, 1)
+        @pl.loop(0, 2)
+        def _(m):
+            rows = pl.ds(pl.multiple_of(FROM[part] + m * (WIDE[part] // 2), 64), WIDE[part] // 2)
+            acc[rows, :] += product(rows, 1)
+
         y_send(part)
-    for part in range(4):
+        if part == 2:
+            z_send(0)
+    for part in (1, 2, 3):
         z_send(part)
-        if part > 0:
-            finish(part - 1)
+        finish(part - 1)
     finish(3)
 
     for unit in range(GROUPS + 2):
@@ -309,8 +314,8 @@
             vmem((SECTORS, 16, GL), BF16), vmem((SECTORS, 16, GL), BF16), vmem((SECTORS, N1, W1), BF16),
             vmem((2, SECTORS, 16, GL), BF16), vmem((SECTORS, N1, W1), BF16),
             vmem((2, V, W1 * CHIPS), BF16), vmem((PA, KL), BF16), vmem((PA, V), F32), vmem((16, PA), F32),
-            vmem((4, 4, 48, 768), F32), vmem((4, 4, 48, 768), BF16), vmem((4, 3, 48, 768), BF16),
-            vmem((4, 4, 16, 768), F32), vmem((4, 4, 16, 768), BF16), vmem((4, 3, 16, 768), BF16),
+            vmem((4, 4, 48, 896), F32), vmem((4, 4, 48, 896), BF16), vmem((4, 3, 48, 896), BF16),
+            vmem((4, 4, 16, 896), F32), vmem((4, 4, 16, 896), BF16), vmem((4, 3, 16, 896), BF16),
             pltpu.SemaphoreType.DMA((2 * GROUPS + 1,)),
             pltpu.SemaphoreType.DMA((GROUPS + 2, CHIPS)), pltpu.SemaphoreType.DMA((3,)),
             pltpu.SemaphoreType.DMA((3, SECTORS)), pltpu.SemaphoreType.DMA((GROUPS + 2,)),

time: 84.2 us -> 83.5 us (level)
  Pallas kernels: 82.3 us -> 81.1 us
    pallas_call x1, Pallas kernels: 82.3 us -> 81.1 us  [update_of(): pl.pallas_call(kernel, out_shape=jax.ShapeDtypeStruct((R0 + R1, PA), F32)...]
where the time goes in v6:
time: 83.5 us; the launch traced here: 82.8 us
  Pallas kernels  81.1 us (97%)
  local copies, waits for them, and re-layouts  1.74 us (2%)
    pallas_call x1, Pallas kernels, update_of(): pl.pallas_call(kernel, out_shape=jax.ShapeDtypeStruct((R0 + R1, PA), F32)...  81.1 us
    reshape x1, local copies, waits for them, and re-layouts, on_device(): return update.reshape(1, R0 + R1, PAIRS, V)  1.74 us

profile of v6, /device:TPU:6, one launch (start us, length us, event | category | flops | bytes accessed | tf_op | source)
XLA Modules:
  0.0 82.8 jit_solution(13348185069376179704)
XLA Ops:
  0.0 81.1 %shard_map.73 = f32[11,2816]{1,0:T(8,128)} custom-call(s32[16]{0:T(128)} %kb_ref.1, s32[2,16]{1,0:T(2,128)} %bitcast.7, f32[32]{0:T(128)} %occ_ref.1, f32[16,176]{1,0:T(8,128)} %own_vir_ref.1, f32[16,176]{1,0:T(8,128)} %own_vir_ref.1, bf16[5632,176]{1,0:T(8,128)(2,1)} %bitcast.4, bf16[32,176,176]{2,1,0:T(8,128)(2,1)} %bitcast.5, bf16[16,176,176]{2,1,0:T(8,128)(2,1)} %bitcast.6), custom_call_target="tpu_custom_call" | custom-call | tf_op jit(solution)/shard_map/pallas_call | solution.py:305
  81.1 1.7 %reshape.15 = f32[1,11,16,176]{3,2,1,0:T(8,128)} reshape(f32[11,2816]{1,0:T(8,128)} %shard_map.73) | data formatting | bytes 247808 | tf_op jit(solution)/shard_map/reshape | solution.py:336

commit v7 on v6

--- a/solution.py
+++ b/solution.py
@@ -189,6 +189,24 @@
 
     start_second(1)
 
+    def sent_first():
+        for unit in range(GROUPS + 2):
+            @pl.when(core != unit % 2)
+            def _():
+                first(unit, 0, True).wait_send()
+
+            for s in range(1, CHIPS):
+                first(unit, s, True).wait_send()
+
+    def sent_second(which):
+        for t in range(2):
+            @pl.when(core != t)
+            def _():
+                second(which, 0, t, True).wait_send()
+
+            for s in range(1, CHIPS):
+                second(which, s, t, True).wait_send()
+
     def arrive(half):
         for g in range(2):
             part = recv.at[half, pl.ds(0, N0), pl.ds(g * GL, GL)]
@@ -254,11 +272,15 @@
         total = zsum[part, z, :, :w]
         for s in range(3):
             total = total + zrecv[part, s, :, :w].astype(F32)
-        o_ref[:, at:at + w] = total[:R0 + R1] / den[:R0 + R1, at:at + w]
+        den[:R0 + R1, at:at + w] = total[:R0 + R1] / den[:R0 + R1, at:at + w]
+        for p in range(PAIRS):
+            if at < (p + 1) * V <= at + w:
+                o_ref[:, p, :] = den[:R0 + R1, p * V:(p + 1) * V]
 
     full[...] = jnp.zeros_like(full)
     zsum[...] = jnp.zeros_like(zsum)
 
+    sent_first()
     arrive(0)
 
     @pl.loop(0, 4)
@@ -266,6 +288,8 @@
         rows = pl.ds(pl.multiple_of(m * (PA // 4), 16), PA // 4)
         acc[rows, :] = product(rows, 0)
 
+    sent_second(0)
+    sent_second(2)
     arrive(1)
     for part in range(4):
         @pl.loop(0, 2)
@@ -276,26 +300,11 @@
         y_send(part)
         if part == 2:
             z_send(0)
+    sent_second(1)
     for part in (1, 2, 3):
         z_send(part)
         finish(part - 1)
     finish(3)
-
-    for unit in range(GROUPS + 2):
-        @pl.when(core != unit % 2)
-        def _():
-            first(unit, 0, True).wait_send()
-
-        for s in range(1, CHIPS):
-            first(unit, s, True).wait_send()
-    for which in range(3):
-        for t in range(2):
-            @pl.when(core != t)
-            def _():
-                second(which, 0, t, True).wait_send()
-
-            for s in range(1, CHIPS):
-                second(which, s, t, True).wait_send()
 
 
 def update_of(kb_table, pair_list, occ_energy, vir_energy, left, right, amps):
@@ -304,7 +313,7 @@
     vmem = pltpu.VMEM
     return pl.pallas_call(
         kernel,
-        out_shape=jax.ShapeDtypeStruct((R0 + R1, PA), F32),
+        out_shape=jax.ShapeDtypeStruct((R0 + R1, PAIRS, V), F32),
         in_specs=[smem] * 4 + [pl.BlockSpec(memory_space=pltpu.VMEM)] + [any_space] * 3,
         out_specs=pl.BlockSpec(memory_space=pltpu.VMEM),
         scratch_shapes=[

time: 83.5 us -> 83.6 us (level)
    reshape x1 -> x0, local copies, waits for them, and re-layouts: 1.74 us -> none  [on_device(): return update.reshape(1, R0 + R1, PAIRS, V)]
    unnamed x0 -> x1, local copies, waits for them, and re-layouts: none -> 1.61 us
where the time goes in v7:
time: 83.6 us; the launch traced here: 82.5 us
  Pallas kernels  80.9 us (97%)
  local copies, waits for them, and re-layouts  1.61 us (2%)
    pallas_call x1, Pallas kernels, update_of(): pl.pallas_call(kernel, out_shape=jax.ShapeDtypeStruct((R0 + R1, PAIRS, V)...  80.9 us

profile of v7, /device:TPU:6, one launch (start us, length us, event | category | flops | bytes accessed | tf_op | source)
XLA Modules:
  0.0 82.5 jit_solution(10729207690998821838)
XLA Ops:
  0.0 80.9 %shard_map.73 = f32[11,16,176]{2,1,0:T(8,128)} custom-call(s32[16]{0:T(128)} %kb_ref.1, s32[2,16]{1,0:T(2,128)} %bitcast.9, f32[32]{0:T(128)} %occ_ref.1, f32[16,176]{1,0:T(8,128)} %own_vir_ref.1, f32[16,176]{1,0:T(8,128)} %own_vir_ref.1, bf16[5632,176]{1,0:T(8,128)(2,1)} %bitcast.5, bf16[32,176,176]{2,1,0:T(8,128)(2,1)} %bitcast.6, ...), custom_call_target="tpu_custom_call" | custom-call | tf_op jit(solution)/shard_map/pallas_call | solution.py:314
  80.9 1.6 %copy.9 = f32[1,11,16,176]{3,2,1,0:T(8,128)} copy(f32[1,11,16,176]{3,2,1,0:T(8,128)} %bitcast.8) | data formatting | bytes 247808
